TPU v7x, 32 devices: a whole 2x2x4 slice. The times are simulated.
32 devices in a mesh: dp: 8 (over y, x, core), ctx: 4 (over z).
Axes of the slice: x: 2, y: 2, z: 4, core: 2. Of those that a mesh axis runs over, the one named last changes fastest.
Arguments:
- tokens: bfloat16 [32, 512, 1024], P('dp', 'ctx'), may hold values from -6 to 6
- cotangent: bfloat16 [32, 512, 1024], P('dp', 'ctx'), may hold values from -6 to 6
- counts: int32 [8], P('dp'), may hold values from 1 to 4, as said below
- block_order: int32 [32, 4], P('dp'), may hold values from 0 to 3, each once within a row
- qkv_weight: float32 [1024, 3072], P(('dp', 'ctx')), may hold values from -0.25 to 0.25
- qkv_first: float32 [1024, 3072], P(('dp', 'ctx')), may hold values from -64 to 64
- qkv_second: float32 [1024, 3072], P(('dp', 'ctx')), may hold values from 557.056 to 2211.84
- proj_weight: float32 [1024, 1024], P(('dp', 'ctx')), may hold values from -1 to 1
- proj_first: float32 [1024, 1024], P(('dp', 'ctx')), may hold values from -10 to 10
- proj_second: float32 [1024, 1024], P(('dp', 'ctx')), may hold values from 14.7456 to 58.9824
- up_weight: float32 [1024, 4096], P(('dp', 'ctx')), may hold values from -0.1875 to 0.1875
- up_first: float32 [1024, 4096], P(('dp', 'ctx')), may hold values from -20 to 20
- up_second: float32 [1024, 4096], P(('dp', 'ctx')), may hold values from 45.8752 to 181.8624
- down_weight: float32 [4096, 1024], P(('dp', 'ctx')), may hold values from -0.09375 to 0.09375
- down_first: float32 [4096, 1024], P(('dp', 'ctx')), may hold values from -40 to 40
- down_second: float32 [4096, 1024], P(('dp', 'ctx')), may hold values from 175.3088 to 697.9584
- vectors: float32 [12, 1024], P(None, ('dp', 'ctx')), may hold values from -1.5 to 1.5, as said below
- vectors_first: float32 [12, 1024], P(None, ('dp', 'ctx')), may hold values from -80 to 80
- vectors_second: float32 [12, 1024], P(None, ('dp', 'ctx')), may hold values from 861.7984 to 3440.64
Outputs:
- layer_out: bfloat16 [32, 512, 1024], P('dp', 'ctx')
- token_grad: float32 [32, 512, 1024], P('dp', 'ctx')
- qkv_new: float32 [1024, 3072], P(('dp', 'ctx'))
- qkv_mean: float32 [1024, 3072], P(('dp', 'ctx'))
- qkv_square: float32 [1024, 3072], P(('dp', 'ctx'))
- proj_new: float32 [1024, 1024], P(('dp', 'ctx'))
- proj_mean: float32 [1024, 1024], P(('dp', 'ctx'))
- proj_square: float32 [1024, 1024], P(('dp', 'ctx'))
- up_new: float32 [1024, 4096], P(('dp', 'ctx'))
- up_mean: float32 [1024, 4096], P(('dp', 'ctx'))
- up_square: float32 [1024, 4096], P(('dp', 'ctx'))
- down_new: float32 [4096, 1024], P(('dp', 'ctx'))
- down_mean: float32 [4096, 1024], P(('dp', 'ctx'))
- down_square: float32 [4096, 1024], P(('dp', 'ctx'))
- vectors_new: float32 [12, 1024], P(None, ('dp', 'ctx'))
- vectors_mean: float32 [12, 1024], P(None, ('dp', 'ctx'))
- vectors_square: float32 [12, 1024], P(None, ('dp', 'ctx'))
Inputs may be any that keep to these rules, and one draw needn't show every extreme that they name: Some group holds 4 live sequences; slot s is live where s % 4 < counts[s // 4]. Each row is a permutation: ctx device c holds the positions block_order[s, c] * 128 to block_order[s, c] * 128 + 127 of sequence s. `vectors`: rows 0 and 5 are the norms' gains, the other rows biases.
All inputs are finite; a program needn't handle non-finite values.
Results may differ from a plain program's by a relative error of at most 0.013.
The roundings to bfloat16 on the way count: a program that leaves them out, or rounds other values in their place, can miss the bound.
Values may be sent and summed in bfloat16 or wider, within the bound.
A program may use at most 192 MiB of HBM per device.

v0:
```python
import jax
import jax.numpy as jnp
from jax import lax
from jax.sharding import PartitionSpec as P

HEAD_DIM = 64
STEP = 10


beta_one = 0.9
beta_two = 0.95
epsilon = 1e-08
weight_decay = 0.1
rate_matrix = 0.1
rate_output = 0.5
rate_vector = 0.4
norm_eps = 1e-05


def layer_norm(values, gain, shift):
    center = values - jnp.mean(values, -1, keepdims=True)
    variance = jnp.mean(center * center, -1, keepdims=True)
    return center * lax.rsqrt(variance + norm_eps) * gain + shift


def gelu_tanh(values):
    return (
        0.5
        * values
        * (1.0 + jnp.tanh(0.7978845608 * (values + 0.044715 * values * values * values)))
    )


def adam_update(weight, first, second, grad, rate, decay_now):
    first_new = beta_one * first + (1.0 - beta_one) * grad
    second_new = beta_two * second + (1.0 - beta_two) * grad * grad
    step_size = (
        first_new
        / (1.0 - beta_one**STEP)
        / (jnp.sqrt(second_new / (1.0 - beta_two**STEP)) + epsilon)
    )
    return (weight - rate * (step_size + decay_now * weight), first_new, second_new)


def shards(
    tokens,
    cotangent,
    counts,
    block_order,
    qkv_weight,
    qkv_first,
    qkv_second,
    proj_weight,
    proj_first,
    proj_second,
    up_weight,
    up_first,
    up_second,
    down_weight,
    down_first,
    down_second,
    vectors,
    vectors_first,
    vectors_second,
):
    slots, span, width = tokens.shape
    blocks = lax.axis_size("ctx")
    length = span * blocks
    heads = width // HEAD_DIM
    rows = slots * span
    scale = HEAD_DIM ** (-0.5)
    full_qkv, full_proj, full_up, full_down, full_table = (
        lax.all_gather(qkv_weight.astype(jnp.bfloat16), ("dp", "ctx"), axis=0, tiled=True),
        lax.all_gather(proj_weight.astype(jnp.bfloat16), ("dp", "ctx"), axis=0, tiled=True),
        lax.all_gather(up_weight.astype(jnp.bfloat16), ("dp", "ctx"), axis=0, tiled=True),
        lax.all_gather(down_weight.astype(jnp.bfloat16), ("dp", "ctx"), axis=0, tiled=True),
        lax.all_gather(vectors.astype(jnp.bfloat16), ("dp", "ctx"), axis=1, tiled=True),
    )
    table = full_table.astype(jnp.float32)
    up_bias = table[8:].reshape(-1)
    live = jnp.where(jnp.arange(slots) < counts[0], 1.0, 0.0).astype(jnp.float32)
    live_rows = jnp.repeat(live, span)[:, None]
    offsets = jnp.arange(span, dtype=jnp.int32)
    own_block = lax.dynamic_index_in_dim(block_order, lax.axis_index("ctx"), 1, keepdims=False)
    query_pos = own_block[:, None] * span + offsets[None, :]
    key_pos = (block_order[:, :, None] * span + offsets[None, None, :]).reshape(slots, length)
    allowed = key_pos[:, None, None, :] <= query_pos[:, None, :, None]
    flat = tokens.reshape(rows, width).astype(jnp.float32)
    normed_full, norm_pull = jax.vjp(layer_norm, flat, table[0], table[1])
    normed = normed_full.astype(jnp.bfloat16)
    mixed = jnp.dot(normed, full_qkv, preferred_element_type=jnp.float32)
    queries = (mixed[:, :width] + table[2]).astype(jnp.bfloat16)
    keys = mixed[:, width : 2 * width].astype(jnp.bfloat16)
    values = (mixed[:, 2 * width :] + table[3]).astype(jnp.bfloat16)
    all_keys, all_values = (
        lax.all_gather(keys.reshape(slots, span, width), "ctx", axis=1, tiled=True),
        lax.all_gather(values.reshape(slots, span, width), "ctx", axis=1, tiled=True),
    )
    query_heads = queries.reshape(slots, span, heads, HEAD_DIM)
    key_heads = all_keys.reshape(slots, length, heads, HEAD_DIM)
    value_heads = all_values.reshape(slots, length, heads, HEAD_DIM)
    scores = jnp.where(
        allowed,
        jnp.einsum("sqhd,skhd->shqk", query_heads, key_heads, preferred_element_type=jnp.float32)
        * scale,
        -1e30,
    )
    top = jnp.max(scores, -1, keepdims=True)
    expd = jnp.exp(scores - top)
    total = jnp.sum(expd, -1, keepdims=True)
    attention_low = (expd / total).astype(jnp.bfloat16)
    log_total = (top + jnp.log(total))[..., 0]
    attended = (
        jnp.einsum(
            "shqk,skhd->sqhd", attention_low, value_heads, preferred_element_type=jnp.float32
        )
        .reshape(rows, width)
        .astype(jnp.bfloat16)
    )
    middle = flat + jnp.dot(attended, full_proj, preferred_element_type=jnp.float32) + table[4]
    normed2_full, norm2_pull = jax.vjp(layer_norm, middle, table[5], table[6])
    normed2 = normed2_full.astype(jnp.bfloat16)
    hidden = jnp.dot(normed2, full_up, preferred_element_type=jnp.float32) + up_bias
    activated, gelu_pull = jax.vjp(gelu_tanh, hidden)
    active = activated.astype(jnp.bfloat16)
    result = middle + jnp.dot(active, full_down, preferred_element_type=jnp.float32) + table[7]
    layer_out = (result * live_rows).astype(jnp.bfloat16).reshape(slots, span, width)
    grad_out = (cotangent.reshape(rows, width).astype(jnp.float32) * live_rows).astype(jnp.bfloat16)
    down_bias_grad = jnp.sum(grad_out.astype(jnp.float32), 0)
    down_grad = jnp.einsum("rf,rd->fd", active, grad_out, preferred_element_type=jnp.float32)
    grad_active = jnp.einsum("rd,fd->rf", grad_out, full_down, preferred_element_type=jnp.float32)
    grad_hidden = gelu_pull(grad_active)[0].astype(jnp.bfloat16)
    up_bias_grad = jnp.sum(grad_hidden.astype(jnp.float32), 0)
    up_grad = jnp.einsum("rd,rf->df", normed2, grad_hidden, preferred_element_type=jnp.float32)
    grad_normed2 = jnp.einsum("rf,df->rd", grad_hidden, full_up, preferred_element_type=jnp.float32)
    back_middle, gain2_grad, shift2_grad = norm2_pull(grad_normed2)
    grad_middle = grad_out.astype(jnp.float32) + back_middle
    grad_branch = grad_middle.astype(jnp.bfloat16)
    proj_bias_grad = jnp.sum(grad_branch.astype(jnp.float32), 0)
    proj_grad = jnp.einsum("rd,re->de", attended, grad_branch, preferred_element_type=jnp.float32)
    grad_attended = jnp.einsum(
        "re,de->rd", grad_branch, full_proj, preferred_element_type=jnp.float32
    ).astype(jnp.bfloat16)
    grad_heads = grad_attended.reshape(slots, span, heads, HEAD_DIM)
    again = jnp.where(
        allowed,
        jnp.einsum("sqhd,skhd->shqk", query_heads, key_heads, preferred_element_type=jnp.float32)
        * scale,
        -1e30,
    )
    attention = jnp.exp(again - log_total[..., None])
    grad_probs = jnp.einsum(
        "sqhd,skhd->shqk", grad_heads, value_heads, preferred_element_type=jnp.float32
    )
    delta = jnp.sum(attention * grad_probs, -1)
    grad_scores = (attention * (grad_probs - delta[..., None])).astype(jnp.bfloat16)
    grad_queries = (
        (
            jnp.einsum(
                "shqk,skhd->sqhd", grad_scores, key_heads, preferred_element_type=jnp.float32
            )
            * scale
        )
        .reshape(rows, width)
        .astype(jnp.bfloat16)
    )
    count = lax.axis_size("ctx") * span
    key_part = (
        jnp.einsum("shqk,sqhd->kshd", grad_scores, query_heads, preferred_element_type=jnp.float32)
        * scale
    )
    value_part = jnp.einsum(
        "shqk,sqhd->kshd", attention_low, grad_heads, preferred_element_type=jnp.float32
    )
    summed = lax.psum_scatter(
        jnp.concatenate(
            (key_part.reshape(count, slots, width), value_part.reshape(count, slots, width)), -1
        ),
        "ctx",
        scatter_dimension=0,
        tiled=True,
    )
    key_grad = jnp.swapaxes(summed[:, :, :width], 0, 1)
    value_grad = jnp.swapaxes(summed[:, :, width:], 0, 1)
    grad_keys = key_grad.reshape(rows, width).astype(jnp.bfloat16)
    grad_values = value_grad.reshape(rows, width).astype(jnp.bfloat16)
    query_bias_grad = jnp.sum(grad_queries.astype(jnp.float32), 0)
    value_bias_grad = jnp.sum(grad_values.astype(jnp.float32), 0)
    grad_mixed = jnp.concatenate((grad_queries, grad_keys, grad_values), -1)
    qkv_grad = jnp.einsum("rd,re->de", normed, grad_mixed, preferred_element_type=jnp.float32)
    grad_normed = jnp.einsum("re,de->rd", grad_mixed, full_qkv, preferred_element_type=jnp.float32)
    back_tokens, gain1_grad, shift1_grad = norm_pull(grad_normed)
    token_grad = (grad_middle + back_tokens).reshape(slots, span, width)
    small_grads = jnp.stack(
        (
            gain1_grad,
            shift1_grad,
            query_bias_grad,
            value_bias_grad,
            proj_bias_grad,
            gain2_grad,
            shift2_grad,
            down_bias_grad,
        )
    )
    table_grad = jnp.concatenate((small_grads, up_bias_grad.reshape(-1, width)), 0)
    qkv_sum, proj_sum, up_sum, down_sum, table_sum = (
        lax.psum_scatter(qkv_grad, ("dp", "ctx"), scatter_dimension=0, tiled=True),
        lax.psum_scatter(proj_grad, ("dp", "ctx"), scatter_dimension=0, tiled=True),
        lax.psum_scatter(up_grad, ("dp", "ctx"), scatter_dimension=0, tiled=True),
        lax.psum_scatter(down_grad, ("dp", "ctx"), scatter_dimension=0, tiled=True),
        lax.psum_scatter(table_grad, ("dp", "ctx"), scatter_dimension=1, tiled=True),
    )
    qkv_new, qkv_mean, qkv_square = adam_update(
        qkv_weight, qkv_first, qkv_second, qkv_sum, rate_matrix, weight_decay
    )
    proj_new, proj_mean, proj_square = adam_update(
        proj_weight, proj_first, proj_second, proj_sum, rate_output, weight_decay
    )
    up_new, up_mean, up_square = adam_update(
        up_weight, up_first, up_second, up_sum, rate_matrix, weight_decay
    )
    down_new, down_mean, down_square = adam_update(
        down_weight, down_first, down_second, down_sum, rate_matrix, weight_decay
    )
    vectors_new, vectors_mean, vectors_square = adam_update(
        vectors, vectors_first, vectors_second, table_sum, rate_vector, 0.0
    )
    return (
        layer_out,
        token_grad,
        qkv_new,
        qkv_mean,
        qkv_square,
        proj_new,
        proj_mean,
        proj_square,
        up_new,
        up_mean,
        up_square,
        down_new,
        down_mean,
        down_square,
        vectors_new,
        vectors_mean,
        vectors_square,
    )


def solution(mesh):
    in_specs = (
        P("dp", "ctx", None),
        P("dp", "ctx", None),
        P("dp"),
        P("dp", None),
        P(("dp", "ctx"), None),
        P(("dp", "ctx"), None),
        P(("dp", "ctx"), None),
        P(("dp", "ctx"), None),
        P(("dp", "ctx"), None),
        P(("dp", "ctx"), None),
        P(("dp", "ctx"), None),
        P(("dp", "ctx"), None),
        P(("dp", "ctx"), None),
        P(("dp", "ctx"), None),
        P(("dp", "ctx"), None),
        P(("dp", "ctx"), None),
        P(None, ("dp", "ctx")),
        P(None, ("dp", "ctx")),
        P(None, ("dp", "ctx")),
    )
    out_specs = (
        P("dp", "ctx", None),
        P("dp", "ctx", None),
        P(("dp", "ctx"), None),
        P(("dp", "ctx"), None),
        P(("dp", "ctx"), None),
        P(("dp", "ctx"), None),
        P(("dp", "ctx"), None),
        P(("dp", "ctx"), None),
        P(("dp", "ctx"), None),
        P(("dp", "ctx"), None),
        P(("dp", "ctx"), None),
        P(("dp", "ctx"), None),
        P(("dp", "ctx"), None),
        P(("dp", "ctx"), None),
        P(None, ("dp", "ctx")),
        P(None, ("dp", "ctx")),
        P(None, ("dp", "ctx")),
    )
    return jax.shard_map(shards, mesh=mesh, in_specs=in_specs, out_specs=out_specs, check_vma=False)
```

profile of v0, /device:TPU:0, one launch (start us, length us, event | category | flops | bytes accessed | tf_op | source)
XLA Modules:
  0.0 2058.1 jit_solution(12485118294633034806)
XLA Ops:
  9.8 71.7 %all-gather = bf16[32,32,12]{1,2,0:T(8,128)(2,1)S(1)} all-gather(bf16[1,32,12]{1,2,0:T(8,128)(2,1)S(1)} %convert_bitcast_fusion), channel_id=1, replica_groups=mesh['dp'=8,'ctx'=4] {'dp','ctx'}, dimensions={0}, use_global_device_ids=true | all-gather | bytes 25344 | tf_op jit(solution)/shard_map/all_gather | solution.py:77
  86.5 5.9 fusion.56
  111.8 61.8 %all-gather.12.cloned.1.call-done = bf16[4,512,1024]{2,1,0:T(8,128)(2,1)} async-done(((bf16[4,128,1024]{2,1,0:T(8,128)(2,1)}), bf16[4,512,1024]{2,1,0:T(8,128)(2,1)}) %all-gather.12.cloned.1.call-update) | async-done | bytes 4194320 | tf_op jit(solution)/shard_map/all_gather | solution.py:96
  173.5 6.2 copy.75
  179.8 75.2 %all-gather.10.cloned.1.call-done = bf16[4,512,1024]{2,1,0:T(8,128)(2,1)} async-done(((bf16[4,128,1024]{2,1,0:T(8,128)(2,1)}), bf16[4,512,1024]{2,1,0:T(8,128)(2,1)}) %all-gather.10.cloned.1.call-update) | async-done | bytes 4194320 | tf_op jit(solution)/shard_map/all_gather | solution.py:97
  254.9 6.2 copy.73
  272.0 5.1 divide_convert_fusion
  277.0 6.5 fusion.22
  285.4 28.0 %all-gather.14.cloned.1.call-done = bf16[1024,1024]{1,0:T(8,128)(2,1)} async-done(((bf16[32,1024]{1,0:T(8,128)(2,1)}), bf16[1024,1024]{1,0:T(8,128)(2,1)}) %all-gather.14.cloned.1.call-update) | async-done | bytes 2097168 | tf_op jit(solution)/shard_map/all_gather | solution.py:74
  317.1 75.9 %all-gather.16.cloned.1.call-done = bf16[1024,4096]{1,0:T(8,128)(2,1)} async-done(((bf16[32,4096]{1,0:T(8,128)(2,1)}), bf16[1024,4096]{1,0:T(8,128)(2,1)}) %all-gather.16.cloned.1.call-update) | async-done | bytes 8388624 | tf_op jit(solution)/shard_map/all_gather | solution.py:75
  393.0 7.3 fusion.42
  403.5 10.1 fusion.43
  413.7 362.9 %reduce-scatter.17.cloned.1.call-done = f32[128,1024]{1,0:T(8,128)} async-done(((f32[4096,1024]{1,0:T(8,128)}), f32[128,1024]{1,0:T(8,128)}) %reduce-scatter.17.cloned.1.call-update) | async-done | bytes 524304 | tf_op jit(solution)/shard_map/reduce_scatter | solution.py:211
  779.9 75.6 %all-gather.18.cloned.1.call-done = bf16[4096,1024]{1,0:T(8,128)(2,1)} async-done(((bf16[128,1024]{1,0:T(8,128)(2,1)}), bf16[4096,1024]{1,0:T(8,128)(2,1)}) %all-gather.18.cloned.1.call-update) | async-done | bytes 8388624 | tf_op jit(solution)/shard_map/all_gather | solution.py:76
  855.4 14.6 convert_reduce_fusion
  870.1 9.5 multiply_reduce_fusion.1
  893.1 8.2 fusion.57
  901.3 8.7 copy.84
  910.1 13.2 multiply_reduce_fusion
  923.3 11.9 multiply_convert_fusion
  940.9 8.7 copy.83
  949.7 11.7 pad_maximum_fusion
  966.3 10.8 fusion.41
  979.3 8.7 convert_reduce_fusion.5
  991.3 249.1 %reduce-scatter.9.cloned.1.call-done = f32[128,4,2048]{2,0,1:T(8,128)} async-done(((f32[512,4,2048]{2,0,1:T(8,128)}), f32[128,4,2048]{2,0,1:T(8,128)}) %reduce-scatter.9.cloned.1.call-update) | async-done | bytes 4194320 | tf_op jit(solution)/shard_map/reduce_scatter | solution.py:175
  1250.5 7.3 fusion.44
  1261.7 10.2 fusion.24
  1272.6 12.3 multiply_convert_fusion.4
  1284.9 106.3 %reduce-scatter.13.cloned.1.call-done = f32[32,1024]{1,0:T(8,128)} async-done(((f32[1024,1024]{1,0:T(8,128)}), f32[32,1024]{1,0:T(8,128)}) %reduce-scatter.13.cloned.1.call-update) | async-done | bytes 131088 | tf_op jit(solution)/shard_map/reduce_scatter | solution.py:209
  1397.1 359.2 %reduce-scatter.15.cloned.1.call-done = f32[32,4096]{1,0:T(8,128)} async-done(((f32[1024,4096]{1,0:T(8,128)}), f32[32,4096]{1,0:T(8,128)}) %reduce-scatter.15.cloned.1.call-update) | async-done | bytes 524304 | tf_op jit(solution)/shard_map/reduce_scatter | solution.py:210
  1758.7 131.9 %reduce-scatter.19.cloned.1.call-done = f32[32,12]{1,0:T(8,128)} async-done(((f32[1024,12]{1,0:T(8,128)}), f32[32,12]{1,0:T(8,128)}) %reduce-scatter.19.cloned.1.call-update) | async-done | bytes 1552
  1892.1 156.5 %reduce-scatter.11.cloned.1.call-done = f32[32,3072]{1,0:T(8,128)} async-done(((f32[1024,3072]{1,0:T(8,128)}), f32[32,3072]{1,0:T(8,128)}) %reduce-scatter.11.cloned.1.call-update) | async-done | bytes 393232 | tf_op jit(solution)/shard_map/reduce_scatter | solution.py:208
  (179 shorter events, 105.4 us)
Async XLA Ops:
  7.2 78.8 %copy-start.3 = (bf16[4,128,1024]{2,1,0:T(8,128)(2,1)S(1)}, bf16[4,128,1024]{2,1,0:T(8,128)(2,1)}, u32[]{:S(2)}) copy-start(bf16[4,128,1024]{2,1,0:T(8,128)(2,1)} %param.19) | copy-start | bytes 3145732
  7.2 79.3 %all-gather.8.cloned.1.call-start = ((), (), s32[]{:S(2)}) async-start(), calls=%async_computation.6 | async-start | bytes 6488064 | tf_op jit(solution)/shard_map/all_gather | solution.py:73
  9.0 164.5 %all-gather.12.cloned.1.call-start = ((), (), s32[]{:S(2)}) async-start(), calls=%async_computation.8 | async-start | bytes 5242880 | tf_op jit(solution)/shard_map/all_gather | solution.py:96
  83.2 9.2 copy-start.27
  96.3 158.7 %all-gather.10.cloned.1.call-start = ((), (), s32[]{:S(2)}) async-start(), calls=%async_computation.7 | async-start | bytes 5242880 | tf_op jit(solution)/shard_map/all_gather | solution.py:97
  100.2 213.2 %all-gather.14.cloned.1.call-start = ((), (), s32[]{:S(2)}) async-start(), calls=%async_computation.9 | async-start | bytes 2162688 | tf_op jit(solution)/shard_map/all_gather | solution.py:74
  100.9 292.1 %all-gather.16.cloned.1.call-start = ((), (), s32[]{:S(2)}) async-start(), calls=%async_computation.10 | async-start | bytes 8650752 | tf_op jit(solution)/shard_map/all_gather | solution.py:75
  102.8 673.7 %reduce-scatter.17.cloned.1.call-start = ((), (), s32[]{:S(2)}) async-start(), calls=%async_computation.16 | async-start | bytes 17301504 | tf_op jit(solution)/shard_map/reduce_scatter | solution.py:211
  111.8 149.4 %copy-start.7 = (bf16[4,128,16,64]{1,3,2,0:T(8,128)(2,1)}, bf16[4,128,16,64]{1,3,2,0:T(8,128)(2,1)S(1)}, u32[]{:S(2)}) copy-start(bf16[4,128,16,64]{1,3,2,0:T(8,128)(2,1)S(1)} %copy.76) | copy-start | bytes 3145732
  313.4 79.6 %copy-start.34 = (f32[1,1024]{1,0:T(1,128)S(1)}, f32[1,1024]{1,0:T(1,128)}, u32[]{:S(2)}) copy-start(f32[1,1024]{1,0:T(1,128)} %get-tuple-element.50) | copy-start | bytes 12292
  313.4 79.6 %copy-start.39 = (f32[1,1024]{1,0:T(1,128)S(1)}, f32[1,1024]{1,0:T(1,128)}, u32[]{:S(2)}) copy-start(f32[1,1024]{1,0:T(1,128)} %get-tuple-element.52) | copy-start | bytes 12292
  393.0 10.5 copy-start.14
  393.0 10.5 copy-start.33
  413.6 441.8 %all-gather.18.cloned.1.call-start = ((), (), s32[]{:S(2)}) async-start(), calls=%async_computation.11 | async-start | bytes 8650752 | tf_op jit(solution)/shard_map/all_gather | solution.py:76
  779.8 460.6 %reduce-scatter.9.cloned.1.call-start = ((), (), s32[]{:S(2)}) async-start(), calls=%async_computation.12 | async-start | bytes 20971520 | tf_op jit(solution)/shard_map/reduce_scatter | solution.py:175
  870.1 9.5 copy-start.42
  923.3 11.9 copy-start.8
  961.4 429.7 %reduce-scatter.13.cloned.1.call-start = ((), (), s32[]{:S(2)}) async-start(), calls=%async_computation.14 | async-start | bytes 4325376 | tf_op jit(solution)/shard_map/reduce_scatter | solution.py:209
  966.2 790.1 %reduce-scatter.15.cloned.1.call-start = ((), (), s32[]{:S(2)}) async-start(), calls=%async_computation.15 | async-start | bytes 17301504 | tf_op jit(solution)/shard_map/reduce_scatter | solution.py:210
  977.1 913.6 %reduce-scatter.19.cloned.1.call-start = ((), (), s32[]{:S(2)}) async-start(), calls=%async_computation.17 | async-start | bytes 540672
  991.3 259.2 %copy-start.23 = (f32[1,1024]{1,0:T(1,128)S(1)}, f32[1,1024]{1,0:T(1,128)}, u32[]{:S(2)}) copy-start(f32[1,1024]{1,0:T(1,128)} %copy-done.22) | copy-start | bytes 12292
  991.3 259.2 %copy-start.28 = (f32[512]{0:T(512)S(1)}, f32[512]{0:T(512)}, u32[]{:S(2)}) copy-start(f32[512]{0:T(512)} %copy-done.27) | copy-start | bytes 6148
  1261.4 787.2 %reduce-scatter.11.cloned.1.call-start = ((), (), s32[]{:S(2)}) async-start(), calls=%async_computation.13 | async-start | bytes 12976128 | tf_op jit(solution)/shard_map/reduce_scatter | solution.py:208
  1272.6 118.6 %copy-start.20 = (f32[32,1024]{1,0:T(8,128)S(1)}, f32[32,1024]{1,0:T(8,128)}, u32[]{:S(2)}) copy-start(f32[32,1024]{1,0:T(8,128)} %param.26) | copy-start | bytes 393220
  1272.6 118.6 %copy-start.21 = (f32[32,1024]{1,0:T(8,128)S(1)}, f32[32,1024]{1,0:T(8,128)}, u32[]{:S(2)}) copy-start(f32[32,1024]{1,0:T(8,128)} %param.27) | copy-start | bytes 393220
  1392.9 363.4 %copy-start.11 = (f32[32,4096]{1,0:T(8,128)S(1)}, f32[32,4096]{1,0:T(8,128)}, u32[]{:S(2)}) copy-start(f32[32,4096]{1,0:T(8,128)} %param.29) | copy-start | bytes 1572868
  1392.9 363.4 %copy-start.17 = (f32[32,4096]{1,0:T(8,128)S(1)}, f32[32,4096]{1,0:T(8,128)}, u32[]{:S(2)}) copy-start(f32[32,4096]{1,0:T(8,128)} %param.30) | copy-start | bytes 1572868
  1392.9 363.4 %copy-start.18 = (f32[32,4096]{1,0:T(8,128)S(1)}, f32[32,4096]{1,0:T(8,128)}, u32[]{:S(2)}) copy-start(f32[32,4096]{1,0:T(8,128)} %param.31) | copy-start | bytes 1572868
  1392.9 498.5 %copy-start.24 = (f32[12,32]{1,0:T(8,128)S(1)}, f32[12,32]{1,0:T(8,128)}, u32[]{:S(2)}) copy-start(f32[12,32]{1,0:T(8,128)} %param.35) | copy-start | bytes 4612
  1392.9 498.5 %copy-start.35 = (f32[12,32]{1,0:T(8,128)S(1)}, f32[12,32]{1,0:T(8,128)}, u32[]{:S(2)}) copy-start(f32[12,32]{1,0:T(8,128)} %param.36) | copy-start | bytes 4612
  1392.9 498.5 %copy-start.36 = (f32[12,32]{1,0:T(8,128)S(1)}, f32[12,32]{1,0:T(8,128)}, u32[]{:S(2)}) copy-start(f32[12,32]{1,0:T(8,128)} %param.37) | copy-start | bytes 4612
  1392.9 655.6 %copy-start.13 = (f32[32,3072]{1,0:T(8,128)S(1)}, f32[32,3072]{1,0:T(8,128)}, u32[]{:S(2)}) copy-start(f32[32,3072]{1,0:T(8,128)} %param.23) | copy-start | bytes 1179652
  (24 other events, 99.5 us)
Sparse Core Ops, SparseCore 0:
  11.5 72.0 all-gather.7
  96.4 77.0 all-gather.11
  175.7 79.2 all-gather.9
  258.3 55.0 all-gather.13
  316.7 76.2 all-gather.15
  413.7 362.7 reduce-scatter.16
  780.1 75.3 all-gather.17
  961.5 278.8 reduce-scatter.8
  1242.8 148.2 reduce-scatter.12
  1393.4 362.8 reduce-scatter.14
  1758.6 131.9 reduce-scatter.18
  1896.5 152.0 reduce-scatter.10
where the time goes:
time: 2060 us
  waiting for transfers between devices  1680 us (82%)
  matrix products  145 us (7%)
  local copies, waits for them, and re-layouts  73.9 us (4%)
  blocking collectives  71.7 us (3%)
  other arithmetic  68.3 us (3%)
    reduce_scatter x1, waiting for transfers between devices, shards(): lax.psum_scatter(down_grad, ('dp', 'ctx'), scatter_dimension=0, tiled=True)  363 us
    reduce_scatter x1, waiting for transfers between devices, shards(): lax.psum_scatter(up_grad, ('dp', 'ctx'), scatter_dimension=0, tiled=True)  359 us
    reduce_scatter x1, waiting for transfers between devices, shards(): lax.psum_scatter(jnp.concatenate((key_part.reshape(count, slots, width),...  249 us
    reduce_scatter x1, waiting for transfers between devices, shards(): lax.psum_scatter(qkv_grad, ('dp', 'ctx'), scatter_dimension=0, tiled=True)  156 us
    unnamed x13, waiting for transfers between devices  132 us
    reduce_scatter x1, waiting for transfers between devices, shards(): lax.psum_scatter(proj_grad, ('dp', 'ctx'), scatter_dimension=0, tiled=True)  106 us
    all_gather x1, waiting for transfers between devices, shards(): lax.all_gather(up_weight.astype(jnp.bfloat16), ('dp', 'ctx'), axis=0, til...  75.9 us
    all_gather x1, waiting for transfers between devices, shards(): lax.all_gather(down_weight.astype(jnp.bfloat16), ('dp', 'ctx'), axis=0, t...  75.6 us
  transfers between devices with their start and end apart: 12, of which 11 were waited for; matrix products, arithmetic and copies ran while one was open for 7% of the time, Pallas kernels for 0%

commit v1 on v0

v1 whole, which is shorter than its diff:
```python
import jax
import jax.numpy as jnp
from jax import lax
from jax.experimental import pallas as pl
from jax.experimental.pallas import tpu as pltpu
from jax.sharding import PartitionSpec as P

HEAD_DIM = 64
STEP = 10


beta_one = 0.9
beta_two = 0.95
epsilon = 1e-08
weight_decay = 0.1
rate_matrix = 0.1
rate_output = 0.5
rate_vector = 0.4
norm_eps = 1e-05


def layer_norm(values, gain, shift):
    center = values - jnp.mean(values, -1, keepdims=True)
    variance = jnp.mean(center * center, -1, keepdims=True)
    return center * lax.rsqrt(variance + norm_eps) * gain + shift


def gelu_tanh(values):
    return (
        0.5
        * values
        * (1.0 + jnp.tanh(0.7978845608 * (values + 0.044715 * values * values * values)))
    )


def adam_update(weight, first, second, grad, rate, decay_now):
    first_new = beta_one * first + (1.0 - beta_one) * grad
    second_new = beta_two * second + (1.0 - beta_two) * grad * grad
    step_size = (
        first_new
        / (1.0 - beta_one**STEP)
        / (jnp.sqrt(second_new / (1.0 - beta_two**STEP)) + epsilon)
    )
    return (weight - rate * (step_size + decay_now * weight), first_new, second_new)


def levels():
    return lax.axis_size("dp").bit_length() - 1


def own_bit(bit):
    return (lax.axis_index("dp") // 2**bit) % 2


def swap(array, bit):
    return lax.ppermute(array, "dp", [(d, d ^ (1 << bit)) for d in range(lax.axis_size("dp"))])


def shift(array, by):
    n = lax.axis_size("ctx")
    return lax.ppermute(array, "ctx", [(c, (c + by) % n) for c in range(n)])


def pick(array, index, axis=0):
    return lax.dynamic_index_in_dim(array, index, axis, keepdims=False)


def put(array, piece, index, axis=0):
    return lax.dynamic_update_index_in_dim(array, piece, index, axis)


def to_sequence(array, order):
    n = lax.axis_size("ctx")
    me = lax.axis_index("ctx")
    out = jnp.zeros_like(array)
    out = put(out, pick(array, me), order[me])
    for by in range(1, n):
        got = shift(pick(array, (me + by) % n), by)
        out = put(out, got, order[(me - by) % n])
    return out.reshape(-1, array.shape[-1])


def from_sequence(array, order, slots):
    n = lax.axis_size("ctx")
    me = lax.axis_index("ctx")
    blocks = array.reshape(slots, -1, array.shape[-1])
    out = put(jnp.zeros_like(blocks), pick(blocks, order[me]), me)
    for by in range(1, n):
        got = shift(pick(blocks, order[(me + by) % n]), by)
        out = put(out, got, (me - by) % n)
    return out


def gather_rows(shard):
    rows, columns = shard.shape
    n = lax.axis_size("ctx")
    me = lax.axis_index("ctx")
    k = levels()
    whole = put(jnp.zeros((n, rows, columns), shard.dtype), shard, me)
    for by in range(1, n):
        whole = put(whole, shift(shard, by), (me - by) % n)
    bits = list(range(1, k))
    cut = columns // 256 * 128
    halves = []
    for order, part in ((bits, whole[:, :, :cut]), (bits[::-1], whole[:, :, cut:])):
        done = []
        for bit in order:
            axis = sum(1 for other in done if other > bit)
            got = swap(part, bit)
            done.append(bit)
            shape = part.shape[:axis] + (2,) + part.shape[axis:]
            part = put(put(jnp.zeros(shape, part.dtype), part, own_bit(bit), axis), got, 1 - own_bit(bit), axis)
        halves.append(part)
    mine = jnp.concatenate(halves, -1)
    got = swap(mine, 0)
    axis = k - 1
    shape = mine.shape[:axis] + (2,) + mine.shape[axis:]
    full = put(put(jnp.zeros(shape, mine.dtype), mine, own_bit(0), axis), got, 1 - own_bit(0), axis)
    return full.reshape(-1, columns)


def scatter_product(left, right):
    count, rows = left.shape
    columns = right.shape[1]
    n = lax.axis_size("ctx")
    me = lax.axis_index("ctx")
    k = levels()
    groups = 2 ** (k - 1)
    each = rows // (2 * groups)
    split = left.reshape(count, groups, 2, each)

    def half(index):
        part = pick(split, index, 2).reshape(count, groups * each)
        return jnp.einsum("rd,re->de", part, right, preferred_element_type=jnp.float32)

    got = swap(half(1 - own_bit(0)).astype(jnp.bfloat16), 0)
    total = (half(own_bit(0)) + got.astype(jnp.float32)).astype(jnp.bfloat16)
    total = total.reshape((2,) * (k - 1) + (n, each // n, columns))
    bits = list(range(1, k))
    cut = columns // 256 * 128
    halves = []
    for order, part in ((bits, total[..., :cut]), (bits[::-1], total[..., cut:])):
        left_bits = sorted(bits, reverse=True)
        for bit in order:
            axis = left_bits.index(bit)
            got = swap(pick(part, 1 - own_bit(bit), axis), bit)
            part = (pick(part, own_bit(bit), axis).astype(jnp.float32) + got.astype(jnp.float32)).astype(jnp.bfloat16)
            left_bits.remove(bit)
        halves.append(part)
    part = jnp.concatenate(halves, -1)
    out = pick(part, me).astype(jnp.float32)
    for by in range(1, n):
        out = out + shift(pick(part, (me + by) % n), by).astype(jnp.float32)
    return out


def probabilities(queries, keys, first):
    scores = lax.dot_general(
        queries, keys, (((1,), (1,)), ((), ())), preferred_element_type=jnp.float32
    ) * (HEAD_DIM ** (-0.5))
    row = lax.broadcasted_iota(jnp.int32, scores.shape, 0) + first
    column = lax.broadcasted_iota(jnp.int32, scores.shape, 1)
    scores = jnp.where(column <= row, scores, -1e30)
    expd = jnp.exp(scores - jnp.max(scores, -1, keepdims=True))
    return expd / jnp.sum(expd, -1, keepdims=True)


def attend_kernel(q_ref, k_ref, v_ref, o_ref):
    length = q_ref.shape[0]
    step = length // 2
    outs = []
    for head in range(q_ref.shape[1] // HEAD_DIM):
        lanes = slice(head * HEAD_DIM, (head + 1) * HEAD_DIM)
        parts = []
        for first in range(0, length, step):
            last = first + step
            p = probabilities(q_ref[first:last, lanes], k_ref[:last, lanes], first)
            parts.append(
                jnp.dot(p.astype(jnp.bfloat16), v_ref[:last, lanes], preferred_element_type=jnp.float32)
            )
        outs.append(jnp.concatenate(parts, 0))
    o_ref[...] = jnp.concatenate(outs, 1).astype(o_ref.dtype)


def attend_back_kernel(q_ref, k_ref, v_ref, g_ref, dq_ref, dk_ref, dv_ref):
    length = q_ref.shape[0]
    step = length // 2
    scale = HEAD_DIM ** (-0.5)
    all_q, all_k, all_v = [], [], []
    for head in range(q_ref.shape[1] // HEAD_DIM):
        lanes = slice(head * HEAD_DIM, (head + 1) * HEAD_DIM)
        dqs, dks, dvs = [], [], []
        for first in range(0, length, step):
            last = first + step
            q, g = q_ref[first:last, lanes], g_ref[first:last, lanes]
            k, v = k_ref[:last, lanes], v_ref[:last, lanes]
            p = probabilities(q, k, first)
            dp = lax.dot_general(g, v, (((1,), (1,)), ((), ())), preferred_element_type=jnp.float32)
            ds = (p * (dp - jnp.sum(p * dp, -1, keepdims=True))).astype(jnp.bfloat16)
            low = p.astype(jnp.bfloat16)
            dqs.append(jnp.dot(ds, k, preferred_element_type=jnp.float32) * scale)
            dks.append(
                lax.dot_general(ds, q, (((0,), (0,)), ((), ())), preferred_element_type=jnp.float32)
            )
            dvs.append(
                lax.dot_general(low, g, (((0,), (0,)), ((), ())), preferred_element_type=jnp.float32)
            )
        all_q.append(jnp.concatenate(dqs, 0))
        all_k.append(jnp.concatenate((dks[0] + dks[1][:step], dks[1][step:]), 0) * scale)
        all_v.append(jnp.concatenate((dvs[0] + dvs[1][:step], dvs[1][step:]), 0))
    dq_ref[...] = jnp.concatenate(all_q, 1).astype(dq_ref.dtype)
    dk_ref[...] = jnp.concatenate(all_k, 1).astype(dk_ref.dtype)
    dv_ref[...] = jnp.concatenate(all_v, 1).astype(dv_ref.dtype)


def attend(mixed):
    length, columns = mixed.shape
    width = columns // 3
    pairs = width // 128

    def block(which):
        return pl.BlockSpec((length, 128), lambda h: (0, which * pairs + h))

    return pl.pallas_call(
        attend_kernel,
        grid=(pairs,),
        in_specs=[block(0), block(1), block(2)],
        out_specs=block(0),
        out_shape=jax.ShapeDtypeStruct((length, width), jnp.bfloat16),
        compiler_params=pltpu.CompilerParams(vmem_limit_bytes=48 * 2**20),
        cost_estimate=pl.CostEstimate(
            flops=4 * length * length * width, bytes_accessed=8 * length * width, transcendentals=0
        ),
    )(mixed, mixed, mixed)


def attend_back(mixed, grad):
    length, columns = mixed.shape
    width = columns // 3
    pairs = width // 128

    def block(which):
        return pl.BlockSpec((length, 128), lambda h: (0, which * pairs + h))

    return pl.pallas_call(
        attend_back_kernel,
        grid=(pairs,),
        in_specs=[block(0), block(1), block(2), block(0)],
        out_specs=[block(0)] * 3,
        out_shape=[jax.ShapeDtypeStruct((length, width), jnp.bfloat16)] * 3,
        compiler_params=pltpu.CompilerParams(vmem_limit_bytes=48 * 2**20),
        cost_estimate=pl.CostEstimate(
            flops=10 * length * length * width, bytes_accessed=14 * length * width, transcendentals=0
        ),
    )(mixed, mixed, mixed, grad)


def shards(
    tokens,
    cotangent,
    counts,
    block_order,
    qkv_weight,
    qkv_first,
    qkv_second,
    proj_weight,
    proj_first,
    proj_second,
    up_weight,
    up_first,
    up_second,
    down_weight,
    down_first,
    down_second,
    vectors,
    vectors_first,
    vectors_second,
):
    slots, span, width = tokens.shape
    ranks = lax.axis_size("ctx")
    length = span * ranks
    me = lax.axis_index("ctx")
    pad = 128
    sequence_order = lax.dynamic_index_in_dim(block_order, me, 0, keepdims=False)
    extra = vectors.T.astype(jnp.bfloat16)
    entries = extra.shape[1]
    extra = jnp.pad(extra, ((0, 0), (0, pad - entries)))
    full_qkv = gather_rows(qkv_weight.astype(jnp.bfloat16))
    table_shard = jnp.concatenate((proj_weight.astype(jnp.bfloat16), extra), 1)
    full_ext = gather_rows(table_shard)
    full_up = gather_rows(up_weight.astype(jnp.bfloat16))
    full_down = gather_rows(down_weight.astype(jnp.bfloat16))
    full_proj = full_ext[:, :width]
    table = full_ext[:, width : width + entries].T.astype(jnp.float32)
    up_bias = table[8:].reshape(-1)
    live = jnp.where(me < counts[0], 1.0, 0.0).astype(jnp.float32)
    flat = to_sequence(tokens, sequence_order).astype(jnp.float32)
    grad_out = (to_sequence(cotangent, sequence_order).astype(jnp.float32) * live).astype(jnp.bfloat16)
    normed_full, norm_pull = jax.vjp(layer_norm, flat, table[0], table[1])
    normed = normed_full.astype(jnp.bfloat16)
    bias = jnp.concatenate((table[2], jnp.zeros_like(table[2]), table[3]))
    mixed = (jnp.dot(normed, full_qkv, preferred_element_type=jnp.float32) + bias).astype(jnp.bfloat16)
    attended = attend(mixed)
    middle = flat + jnp.dot(attended, full_proj, preferred_element_type=jnp.float32) + table[4]
    normed2_full, norm2_pull = jax.vjp(layer_norm, middle, table[5], table[6])
    normed2 = normed2_full.astype(jnp.bfloat16)
    hidden = jnp.dot(normed2, full_up, preferred_element_type=jnp.float32) + up_bias
    activated, gelu_pull = jax.vjp(gelu_tanh, hidden)
    active = activated.astype(jnp.bfloat16)
    result = middle + jnp.dot(active, full_down, preferred_element_type=jnp.float32) + table[7]
    layer_out = from_sequence((result * live).astype(jnp.bfloat16), sequence_order, slots)
    down_bias_grad = jnp.sum(grad_out.astype(jnp.float32), 0)
    down_sum = scatter_product(active, grad_out)
    grad_active = jnp.einsum("rd,fd->rf", grad_out, full_down, preferred_element_type=jnp.float32)
    grad_hidden = gelu_pull(grad_active)[0].astype(jnp.bfloat16)
    up_bias_grad = jnp.sum(grad_hidden.astype(jnp.float32), 0)
    up_sum = scatter_product(normed2, grad_hidden)
    grad_normed2 = jnp.einsum("rf,df->rd", grad_hidden, full_up, preferred_element_type=jnp.float32)
    back_middle, gain2_grad, shift2_grad = norm2_pull(grad_normed2)
    grad_middle = grad_out.astype(jnp.float32) + back_middle
    grad_branch = grad_middle.astype(jnp.bfloat16)
    proj_bias_grad = jnp.sum(grad_branch.astype(jnp.float32), 0)
    proj_sum = scatter_product(attended, grad_branch)
    grad_attended = jnp.einsum(
        "re,de->rd", grad_branch, full_proj, preferred_element_type=jnp.float32
    ).astype(jnp.bfloat16)
    grad_queries, grad_keys, grad_values = attend_back(mixed, grad_attended)
    query_bias_grad = jnp.sum(grad_queries.astype(jnp.float32), 0)
    value_bias_grad = jnp.sum(grad_values.astype(jnp.float32), 0)
    grad_mixed = jnp.concatenate((grad_queries, grad_keys, grad_values), -1)
    qkv_sum = scatter_product(normed, grad_mixed)
    grad_normed = jnp.einsum("re,de->rd", grad_mixed, full_qkv, preferred_element_type=jnp.float32)
    back_tokens, gain1_grad, shift1_grad = norm_pull(grad_normed)
    token_grad = from_sequence(
        (grad_middle + back_tokens).astype(jnp.bfloat16), sequence_order, slots
    ).astype(jnp.float32)
    small_grads = jnp.stack(
        (
            gain1_grad,
            shift1_grad,
            query_bias_grad,
            value_bias_grad,
            proj_bias_grad,
            gain2_grad,
            shift2_grad,
            down_bias_grad,
        )
    )
    table_grad = jnp.concatenate((small_grads, up_bias_grad.reshape(-1, width)), 0)
    table_sum = lax.psum_scatter(table_grad, ("dp", "ctx"), scatter_dimension=1, tiled=True)
    qkv_new, qkv_mean, qkv_square = adam_update(
        qkv_weight, qkv_first, qkv_second, qkv_sum, rate_matrix, weight_decay
    )
    proj_new, proj_mean, proj_square = adam_update(
        proj_weight, proj_first, proj_second, proj_sum, rate_output, weight_decay
    )
    up_new, up_mean, up_square = adam_update(
        up_weight, up_first, up_second, up_sum, rate_matrix, weight_decay
    )
    down_new, down_mean, down_square = adam_update(
        down_weight, down_first, down_second, down_sum, rate_matrix, weight_decay
    )
    vectors_new, vectors_mean, vectors_square = adam_update(
        vectors, vectors_first, vectors_second, table_sum, rate_vector, 0.0
    )
    return (
        layer_out,
        token_grad,
        qkv_new,
        qkv_mean,
        qkv_square,
        proj_new,
        proj_mean,
        proj_square,
        up_new,
        up_mean,
        up_square,
        down_new,
        down_mean,
        down_square,
        vectors_new,
        vectors_mean,
        vectors_square,
    )


def solution(mesh):
    in_specs = (
        P("dp", "ctx", None),
        P("dp", "ctx", None),
        P("dp"),
        P("dp", None),
        P(("dp", "ctx"), None),
        P(("dp", "ctx"), None),
        P(("dp", "ctx"), None),
        P(("dp", "ctx"), None),
        P(("dp", "ctx"), None),
        P(("dp", "ctx"), None),
        P(("dp", "ctx"), None),
        P(("dp", "ctx"), None),
        P(("dp", "ctx"), None),
        P(("dp", "ctx"), None),
        P(("dp", "ctx"), None),
        P(("dp", "ctx"), None),
        P(None, ("dp", "ctx")),
        P(None, ("dp", "ctx")),
        P(None, ("dp", "ctx")),
    )
    out_specs = (
        P("dp", "ctx", None),
        P("dp", "ctx", None),
        P(("dp", "ctx"), None),
        P(("dp", "ctx"), None),
        P(("dp", "ctx"), None),
        P(("dp", "ctx"), None),
        P(("dp", "ctx"), None),
        P(("dp", "ctx"), None),
        P(("dp", "ctx"), None),
        P(("dp", "ctx"), None),
        P(("dp", "ctx"), None),
        P(("dp", "ctx"), None),
        P(("dp", "ctx"), None),
        P(("dp", "ctx"), None),
        P(None, ("dp", "ctx")),
        P(None, ("dp", "ctx")),
        P(None, ("dp", "ctx")),
    )
    return jax.shard_map(shards, mesh=mesh, in_specs=in_specs, out_specs=out_specs, check_vma=False)
```

time: 2060 us -> 730 us (0.35)
  waiting for transfers between devices: 1680 us -> 259 us
  local copies, waits for them, and re-layouts: 73.9 us -> 169 us
  starting transfers between devices: 1.14 us -> 95.3 us
  blocking collectives: 71.7 us -> 0 us
  matrix products: 145 us -> 87.8 us
  Pallas kernels: 0 us -> 40.6 us
  other arithmetic: 68.3 us -> 39.2 us
    reduce_scatter x5 -> x0, waiting for transfers between devices: 1230 us -> none  [the longest x1 363 us: shards(): lax.psum_scatter(down_grad, ('dp', 'ctx'), scatter_dimension=0, tiled=True)]
    all_gather x6 -> x0, waiting for transfers between devices: 316 us -> none  [the longest x1 75.9 us: shards(): lax.all_gather(up_weight.astype(jnp.bfloat16), ('dp', 'ctx'), axis=0, til...]
    ppermute x0 -> x76, waiting for transfers between devices: none -> 198 us  [the longest x40 116 us: swap(): lax.ppermute(array, 'dp', [(d, d ^ 1 << bit) for d in range(lax.axis_size...]
    ppermute x0 -> x76, starting transfers between devices: none -> 95.3 us  [the longest x36 62.4 us: shift(): return lax.ppermute(array, 'ctx', [(c, (c + by) % n) for c in range(n)])]
    all_gather x1 -> x0, blocking collectives: 71.7 us -> none  [shards(): lax.all_gather(vectors.astype(jnp.bfloat16), ('dp', 'ctx'), axis=1, tiled...]
    unnamed x13 -> x2, waiting for transfers between devices: 132 us -> 61.1 us
    dynamic_update_slice x0 -> x60, local copies, waits for them, and re-layouts: none -> 52.5 us  [put(): return lax.dynamic_update_index_in_dim(array, piece, index, axis)]
    dot_general x11 -> x9, matrix products: 88.2 us -> 37.6 us  [the longest x8 31 us: half(): jnp.einsum('rd,re->de', part, right, preferred_element_type=jnp.float32)]
  transfers between devices with their start and end apart: 12 -> 77, of which waited for: 11 -> 35; matrix products, arithmetic and copies ran while one was open for 7% -> 33% of each run, Pallas kernels for 0% -> 2%
where the time goes in v1:
time: 730 us; the launch traced here: 722 us
  waiting for transfers between devices  259 us (35%)
  local copies, waits for them, and re-layouts  169 us (23%)
  starting transfers between devices  95.3 us (13%)
  matrix products  87.8 us (12%)
  Pallas kernels  40.6 us (6%)
  other arithmetic  39.2 us (5%)
  between operations  30.7 us (4%)
    ppermute x40, waiting for transfers between devices, swap(): lax.ppermute(array, 'dp', [(d, d ^ 1 << bit) for d in range(lax.axis_size...  116 us
    ppermute x36, waiting for transfers between devices, shift(): return lax.ppermute(array, 'ctx', [(c, (c + by) % n) for c in range(n)])  82.6 us
    ppermute x36, starting transfers between devices, shift(): return lax.ppermute(array, 'ctx', [(c, (c + by) % n) for c in range(n)])  62.4 us
    unnamed x2, waiting for transfers between devices  61.1 us
    dynamic_update_slice x60, local copies, waits for them, and re-layouts, put(): return lax.dynamic_update_index_in_dim(array, piece, index, axis)  52.5 us
    unnamed x180, local copies, waits for them, and re-layouts  47.5 us
    ppermute x40, starting transfers between devices, swap(): lax.ppermute(array, 'dp', [(d, d ^ 1 << bit) for d in range(lax.axis_size...  32.9 us
    dot_general x8, matrix products, half(): jnp.einsum('rd,re->de', part, right, preferred_element_type=jnp.float32)  31 us
  transfers between devices with their start and end apart: 77, of which 35 were waited for; matrix products, arithmetic and copies ran while one was open for 33% of the time, Pallas kernels for 2%

profile of v1, /device:TPU:0, one launch (start us, length us, event | category | flops | bytes accessed | tf_op | source)
XLA Modules:
  0.0 722.1 jit_solution(9859472457414891514)
XLA Ops:
  53.0 6.7 collective-permute-done.12
  82.7 8.7 %collective-permute-done.20 = bf16[32,4096]{1,0:T(8,128)(2,1)S(1)} collective-permute-done((bf16[32,4096]{1,0:T(8,128)(2,1)S(1)}, bf16[32,4096]{1,0:T(8,128)(2,1)S(1)}, u32[]{:S(2)}, u32[]{:S(2)}) %collective-permute-start.20) | collective-permute-done | bytes 262176 | tf_op jit(solution)/shard_map/ppermute | solution.py:61
  110.6 5.3 collective-permute-done.1
  116.4 6.3 collective-permute-done.2
  128.9 8.7 %collective-permute-done.39 = bf16[128,1024]{1,0:T(8,128)(2,1)S(1)} collective-permute-done((bf16[128,1024]{1,0:T(8,128)(2,1)S(1)}, bf16[128,1024]{1,0:T(8,128)(2,1)S(1)}, u32[]{:S(2)}, u32[]{:S(2)}) %collective-permute-start.39) | collective-permute-done | bytes 262176 | tf_op jit(solution)/shard_map/ppermute | solution.py:61
  183.3 8.0 %collective-permute-done.17 = bf16[2,4,32,1536]{3,2,1,0:T(8,128)(2,1)S(1)} collective-permute-done((bf16[2,4,32,1536]{3,2,1,0:T(8,128)(2,1)S(1)}, bf16[2,4,32,1536]{3,2,1,0:T(8,128)(2,1)S(1)}, u32[]{:S(2)}, u32[]{:S(2)}) %collective-permute-start.17) | collective-permute-done | bytes 786464 | tf_op jit(solution)/shard_map/ppermute | solution.py:56
  199.5 14.4 %collective-permute-done.33 = bf16[2,4,128,512]{3,2,1,0:T(8,128)(2,1)} collective-permute-done((bf16[2,4,128,512]{3,2,1,0:T(8,128)(2,1)}, bf16[2,4,128,512]{3,2,1,0:T(8,128)(2,1)}, u32[]{:S(2)}, u32[]{:S(2)}) %collective-permute-start.33) | collective-permute-done | bytes 1048608 | tf_op jit(solution)/shard_map/ppermute | solution.py:56
  219.1 15.6 %collective-permute-done.25 = bf16[2,4,32,2048]{3,2,1,0:T(8,128)(2,1)} collective-permute-done((bf16[2,4,32,2048]{3,2,1,0:T(8,128)(2,1)}, bf16[2,4,32,2048]{3,2,1,0:T(8,128)(2,1)}, u32[]{:S(2)}, u32[]{:S(2)}) %collective-permute-start.25) | collective-permute-done | bytes 1048608 | tf_op jit(solution)/shard_map/ppermute | solution.py:56
  255.5 6.6 add_convert_fusion.3.q_ref.k_ref.v_ref
  262.1 16.2 %shard_map.314 = bf16[512,1024]{1,0:T(8,128)(2,1)S(1)} custom-call(bf16[512,3072]{1,0:T(8,128)(2,1)S(1)} %add_convert_fusion.3.q_ref.k_ref.v_ref, bf16[512,3072]{1,0:T(8,128)(2,1)S(1)} %add_convert_fusion.3.q_ref.k_ref.v_ref, bf16[512,3072]{1,0:T(8,128)(2,1)S(1)} %add_convert_fusion.3.q_ref.k_ref.v_ref), custom_call_target="tpu_custom_call" | custom-call | flops 1073741824 | bytes 4194304 | tf_op jit(solution)/shard_map/pallas_call | solution.py:224
  289.8 7.0 constant_dynamic-slice_fusion.2
  314.5 10.2 %fusion.114 = f32[512,4096]{1,0:T(8,128)} fusion(bf16[512,1024]{1,0:T(8,128)(2,1)S(1)} %copy-done.28, bf16[1024,4096]{1,0:T(8,128)(2,1)} %bitcast.449), kind=kOutput, calls=%fused_computation.342 | convolution fusion | flops 4294967296 | bytes 17825792 | tf_op jit(solution)/shard_map/dot_general | solution.py:307
  327.6 16.6 %convert_reduce_fusion = (f32[4096]{0:T(1024)S(1)}, bf16[512,4096]{1,0:T(8,128)(2,1)S(1)}, bf16[512,4096]{1,0:T(8,128)(2,1)}) fusion(f32[512,4096]{1,0:T(8,128)} %fusion.114, f32[4096]{0:T(1024)S(1)} %bitcast.485, bf16[512,1024]{1,0:T(8,128)(2,1)S(1)} %bitcast.441, bf16[4096,1024]{1,0:T(8,128)(2,1)S(1)} %bitcast.445), kind=kOutput, calls=%fused_computation.10 | convolution fusion | flops 4355780608 | bytes 26247168 | tf_op jit(solution)/shard_map/rd,fd->rf/dot_general | solution.py:314
  344.2 9.0 %multiply_reduce_fusion = (f32[1024]{0:T(1024)S(1)}, f32[512]{0:T(512)S(1)}, f32[1024]{0:T(1024)S(1)}, f32[512,1024]{1,0:T(8,128)S(1)}) fusion(f32[512,1024]{1,0:T(8,128)S(1)} %get-tuple-element.130, f32[512]{0:T(512)S(1)} %fusion.92, f32[512]{0:T(512)S(1)} %broadcast_multiply_fusion, f32[1024]{0:T(1024)S(1)} %get-tuple-element.32, ...), kind=kOutput, calls=%fused_computation.56 | convolution fusion | flops 4299159040 | bytes 16795648 | tf_op jit(solution)/shard_map/rf,df->rd/dot_general | solution.py:318
  358.8 24.4 %shard_map.315 = (bf16[512,1024]{1,0:T(8,128)(2,1)S(1)}, bf16[512,1024]{1,0:T(8,128)(2,1)S(1)}, bf16[512,1024]{1,0:T(8,128)(2,1)S(1)}) custom-call(bf16[512,3072]{1,0:T(8,128)(2,1)} %copy-done, bf16[512,3072]{1,0:T(8,128)(2,1)} %copy-done, bf16[512,3072]{1,0:T(8,128)(2,1)} %copy-done, bf16[512,1024]{1,0:T(8,128)(2,1)S(1)} %fusion.29.g_ref), custom_call_target="tpu_custom_call" | custom-call | flops 2684354560 | bytes 7340032 | tf_op jit(solution)/shard_map/pallas_call | solution.py:245
  385.2 5.0 fusion.96
  394.0 7.8 %reshape.326 = bf16[512,4,2,512]{3,2,1,0:T(2,128)(2,1)} reshape(bf16[512,4096]{1,0:T(8,128)(2,1)} %get-tuple-element.67) | data formatting | bytes 8388608 | tf_op jit(solution)/shard_map/reshape | solution.py:130
  401.8 11.4 %constant_dynamic-slice_fusion = (bf16[512,4,1,512]{3,2,1,0:T(2,128)(2,1)}, bf16[512,4,1,512]{3,2,1,0:T(2,128)(2,1)}) fusion(bf16[512,4,2,512]{3,2,1,0:T(2,128)(2,1)} %reshape.326, s32[]{:T(128)S(6)} %select_n.652, s32[]{:T(128)S(6)} %select_n.651), kind=kLoop, calls=%fused_computation.299 | loop fusion | bytes 8388616 | tf_op jit(solution)/shard_map/jit(dynamic_index_in_dim)/dynamic_slice | solution.py:65
  413.2 10.5 %copy.130 = bf16[512,4,1,512]{0,3,1,2:T(8,128)(2,1)} copy(bf16[512,4,1,512]{3,2,1,0:T(2,128)(2,1)} %get-tuple-element.70) | data formatting | bytes 4194304
  423.7 6.3 convolution_convert_fusion.2
  430.5 10.5 %copy.129 = bf16[512,4,1,512]{0,3,1,2:T(8,128)(2,1)} copy(bf16[512,4,1,512]{3,2,1,0:T(2,128)(2,1)} %get-tuple-element.71) | data formatting | bytes 4194304
  441.0 6.9 convolution_convert_fusion
  469.5 61.0 %reduce-scatter.4.cloned.1.call-done = f32[32,12]{1,0:T(8,128)} async-done(((f32[1024,12]{1,0:T(8,128)}), f32[32,12]{1,0:T(8,128)}) %reduce-scatter.4.cloned.1.call-update) | async-done | bytes 1552
  535.1 6.3 collective-permute-done.43
  546.1 9.9 %collective-permute-done.36 = bf16[128,1024]{1,0:T(8,128)(2,1)S(1)} collective-permute-done((bf16[128,1024]{1,0:T(8,128)(2,1)}, bf16[128,1024]{1,0:T(8,128)(2,1)S(1)}, u32[]{:S(2)}, u32[]{:S(2)}) %collective-permute-start.36) | collective-permute-done | bytes 262176 | tf_op jit(solution)/shard_map/ppermute | solution.py:61
  557.0 7.2 %collective-permute-done.55 = bf16[2,4,32,512]{3,2,1,0:T(8,128)(2,1)S(1)} collective-permute-done((bf16[2,4,32,512]{3,2,1,0:T(8,128)(2,1)S(1)}, bf16[2,4,32,512]{3,2,1,0:T(8,128)(2,1)S(1)}, u32[]{:S(2)}, u32[]{:S(2)}) %collective-permute-start.55) | collective-permute-done | bytes 262176 | tf_op jit(solution)/shard_map/ppermute | solution.py:56
  564.4 7.3 %collective-permute-done.53 = bf16[2,4,32,512]{3,2,1,0:T(8,128)(2,1)S(1)} collective-permute-done((bf16[2,4,32,512]{3,2,1,0:T(8,128)(2,1)S(1)}, bf16[2,4,32,512]{3,2,1,0:T(8,128)(2,1)S(1)}, u32[]{:S(2)}, u32[]{:S(2)}) %collective-permute-start.53) | collective-permute-done | bytes 262176 | tf_op jit(solution)/shard_map/ppermute | solution.py:56
  602.4 12.2 %collective-permute-done.45 = bf16[2,4,32,1536]{3,2,1,0:T(8,128)(2,1)S(1)} collective-permute-done((bf16[2,4,32,1536]{3,2,1,0:T(8,128)(2,1)S(1)}, bf16[2,4,32,1536]{3,2,1,0:T(8,128)(2,1)S(1)}, u32[]{:S(2)}, u32[]{:S(2)}) %collective-permute-start.45) | collective-permute-done | bytes 786464 | tf_op jit(solution)/shard_map/ppermute | solution.py:56
  640.6 8.8 %collective-permute-done.71 = bf16[2,4,128,512]{3,2,1,0:T(8,128)(2,1)S(1)} collective-permute-done((bf16[2,4,128,512]{3,2,1,0:T(8,128)(2,1)S(1)}, bf16[2,4,128,512]{3,2,1,0:T(8,128)(2,1)S(1)}, u32[]{:S(2)}, u32[]{:S(2)}) %collective-permute-start.71) | collective-permute-done | bytes 1048608 | tf_op jit(solution)/shard_map/ppermute | solution.py:56
  652.7 19.1 %collective-permute-done.63 = bf16[2,4,32,2048]{3,2,1,0:T(8,128)(2,1)S(1)} collective-permute-done((bf16[2,4,32,2048]{3,2,1,0:T(8,128)(2,1)S(1)}, bf16[2,4,32,2048]{3,2,1,0:T(8,128)(2,1)S(1)}, u32[]{:S(2)}, u32[]{:S(2)}) %collective-permute-start.63) | collective-permute-done | bytes 1048608 | tf_op jit(solution)/shard_map/ppermute | solution.py:56
  691.3 7.9 %collective-permute-done.74 = bf16[128,1024]{1,0:T(8,128)(2,1)S(1)} collective-permute-done((bf16[128,1024]{1,0:T(8,128)(2,1)S(1)}, bf16[128,1024]{1,0:T(8,128)(2,1)S(1)}, u32[]{:S(2)}, u32[]{:S(2)}) %collective-permute-start.74) | collective-permute-done | bytes 262176 | tf_op jit(solution)/shard_map/ppermute | solution.py:61
  702.1 11.0 %collective-permute-done.66 = bf16[32,4096]{1,0:T(8,128)(2,1)S(1)} collective-permute-done((bf16[32,4096]{1,0:T(8,128)(2,1)S(1)}, bf16[32,4096]{1,0:T(8,128)(2,1)S(1)}, u32[]{:S(2)}, u32[]{:S(2)}) %collective-permute-start.66) | collective-permute-done | bytes 262176 | tf_op jit(solution)/shard_map/ppermute | solution.py:61
  (523 shorter events, 318.6 us)
Async XLA Ops:
  7.2 523.3 %reduce-scatter.4.cloned.1.call-start = ((), (), s32[]{:S(2)}) async-start(), calls=%async_computation.1 | async-start | bytes 540672
  9.3 93.7 %collective-permute-start.27 = (bf16[128,1024]{1,0:T(8,128)(2,1)}, bf16[128,1024]{1,0:T(8,128)(2,1)}, u32[]{:S(2)}, u32[]{:S(2)}) collective-permute-start(bf16[128,1024]{1,0:T(8,128)(2,1)} %get-tuple-element.62), channel_id=1, source_target_pairs={{0,1},{1,2},{2,3},{3,0},{4,5},{5,6},{6,7},{7,4},{8,9},{9,10},{10,1... | collective-permute-start | bytes 786440 | tf_op jit(solution)/shard_map/ppermute | solution.py:61
  12.3 91.7 %collective-permute-start.28 = (bf16[128,1024]{1,0:T(8,128)(2,1)}, bf16[128,1024]{1,0:T(8,128)(2,1)}, u32[]{:S(2)}, u32[]{:S(2)}) collective-permute-start(bf16[128,1024]{1,0:T(8,128)(2,1)} %get-tuple-element.62), channel_id=1, source_target_pairs={{0,2},{1,3},{2,0},{3,1},{4,6},{5,7},{6,4},{7,5},{8,10},{9,11},{10,... | collective-permute-start | bytes 786440 | tf_op jit(solution)/shard_map/ppermute | solution.py:61
  14.9 92.2 %collective-permute-start.29 = (bf16[128,1024]{1,0:T(8,128)(2,1)}, bf16[128,1024]{1,0:T(8,128)(2,1)}, u32[]{:S(2)}, u32[]{:S(2)}) collective-permute-start(bf16[128,1024]{1,0:T(8,128)(2,1)} %get-tuple-element.62), channel_id=1, source_target_pairs={{0,3},{1,0},{2,1},{3,2},{4,7},{5,4},{6,5},{7,6},{8,11},{9,8},{10,9... | collective-permute-start | bytes 786440 | tf_op jit(solution)/shard_map/ppermute | solution.py:61
  17.1 25.6 %collective-permute-start.4 = (bf16[32,1152]{1,0:T(8,128)(2,1)S(1)}, bf16[32,1152]{1,0:T(8,128)(2,1)}, u32[]{:S(2)}, u32[]{:S(2)}) collective-permute-start(bf16[32,1152]{1,0:T(8,128)(2,1)S(1)} %fusion.82), channel_id=1, source_target_pairs={{0,2},{1,3},{2,0},{3,1},{4,6},{5,7},{6,4},{7,5},{8,10},{9,11},{10,... | collective-permute-start | bytes 221192 | tf_op jit(solution)/shard_map/ppermute | solution.py:61
  107.0 30.5 %collective-permute-start.39 = (bf16[128,1024]{1,0:T(8,128)(2,1)S(1)}, bf16[128,1024]{1,0:T(8,128)(2,1)S(1)}, u32[]{:S(2)}, u32[]{:S(2)}) collective-permute-start(bf16[128,1024]{1,0:T(8,128)(2,1)S(1)} %get-tuple-element.97), channel_id=1, source_target_pairs={{0,2},{1,3},{2,0},{3,1},{4,6},{5,7},{6,4},{7,5},{8,10},{9,11},{10,... | collective-permute-start | bytes 786440 | tf_op jit(solution)/shard_map/ppermute | solution.py:61
  108.1 31.1 %collective-permute-start.40 = (bf16[128,1024]{1,0:T(8,128)(2,1)S(1)}, bf16[128,1024]{1,0:T(8,128)(2,1)S(1)}, u32[]{:S(2)}, u32[]{:S(2)}) collective-permute-start(bf16[128,1024]{1,0:T(8,128)(2,1)S(1)} %get-tuple-element.94), channel_id=1, source_target_pairs={{0,3},{1,0},{2,1},{3,2},{4,7},{5,4},{6,5},{7,6},{8,11},{9,8},{10,9... | collective-permute-start | bytes 786440 | tf_op jit(solution)/shard_map/ppermute | solution.py:61
  115.9 39.5 %collective-permute-start.14 = (bf16[4,32,1536]{2,1,0:T(8,128)(2,1)}, bf16[4,32,1536]{2,1,0:T(8,128)(2,1)}, u32[]{:S(2)}, u32[]{:S(2)}) collective-permute-start(bf16[4,32,1536]{2,1,0:T(8,128)(2,1)} %get-tuple-element.113), channel_id=1, source_target_pairs={{0,8},{4,12},{8,0},{12,4},{16,24},{20,28},{24,16},{28,20},{1,9},{5... | collective-permute-start | bytes 1179656 | tf_op jit(solution)/shard_map/ppermute | solution.py:56
  122.7 37.0 %collective-permute-start.16 = (bf16[4,32,1536]{2,1,0:T(8,128)(2,1)S(1)}, bf16[4,32,1536]{2,1,0:T(8,128)(2,1)}, u32[]{:S(2)}, u32[]{:S(2)}) collective-permute-start(bf16[4,32,1536]{2,1,0:T(8,128)(2,1)S(1)} %get-tuple-element.114), channel_id=1, source_target_pairs={{0,16},{4,20},{8,24},{12,28},{16,0},{20,4},{24,8},{28,12},{1,17},{... | collective-permute-start | bytes 1179656 | tf_op jit(solution)/shard_map/ppermute | solution.py:56
  159.7 35.4 %collective-permute-start.10 = (bf16[2,2,4,32,1152]{4,3,2,1,0:T(8,128)(2,1)S(1)}, bf16[2,2,4,32,1152]{4,3,2,1,0:T(8,128)(2,1)S(1)}, u32[]{:S(2)}, u32[]{:S(2)}) collective-permute-start(bf16[2,2,4,32,1152]{4,3,2,1,0:T(8,128)(2,1)S(1)} %pad_maximum_fusion.3), channel_id=1, source_target_pairs={{0,4},{4,0},{8,12},{12,8},{16,20},{20,16},{24,28},{28,24},{1,5},{5... | collective-permute-start | bytes 3538952 | tf_op jit(solution)/shard_map/ppermute | solution.py:56
  166.1 25.1 %collective-permute-start.17 = (bf16[2,4,32,1536]{3,2,1,0:T(8,128)(2,1)S(1)}, bf16[2,4,32,1536]{3,2,1,0:T(8,128)(2,1)S(1)}, u32[]{:S(2)}, u32[]{:S(2)}) collective-permute-start(bf16[2,4,32,1536]{3,2,1,0:T(8,128)(2,1)S(1)} %bitcast_dynamic-update-slice_fusion.28), channel_id=1, source_target_pairs={{0,8},{4,12},{8,0},{12,4},{16,24},{20,28},{24,16},{28,20},{1,9},{5... | collective-permute-start | bytes 2359304 | tf_op jit(solution)/shard_map/ppermute | solution.py:56
  168.5 45.3 %collective-permute-start.33 = (bf16[2,4,128,512]{3,2,1,0:T(8,128)(2,1)}, bf16[2,4,128,512]{3,2,1,0:T(8,128)(2,1)}, u32[]{:S(2)}, u32[]{:S(2)}) collective-permute-start(bf16[2,4,128,512]{3,2,1,0:T(8,128)(2,1)} %bitcast_dynamic-update-slice_fusion.20), channel_id=1, source_target_pairs={{0,8},{4,12},{8,0},{12,4},{16,24},{20,28},{24,16},{28,20},{1,9},{5... | collective-permute-start | bytes 3145736 | tf_op jit(solution)/shard_map/ppermute | solution.py:56
  174.4 40.8 %collective-permute-start.31 = (bf16[2,4,128,512]{3,2,1,0:T(8,128)(2,1)}, bf16[2,4,128,512]{3,2,1,0:T(8,128)(2,1)}, u32[]{:S(2)}, u32[]{:S(2)}) collective-permute-start(bf16[2,4,128,512]{3,2,1,0:T(8,128)(2,1)} %bitcast_dynamic-update-slice_fusion.22), channel_id=1, source_target_pairs={{0,16},{4,20},{8,24},{12,28},{16,0},{20,4},{24,8},{28,12},{1,17},{... | collective-permute-start | bytes 3145736 | tf_op jit(solution)/shard_map/ppermute | solution.py:56
  181.7 52.9 %collective-permute-start.25 = (bf16[2,4,32,2048]{3,2,1,0:T(8,128)(2,1)}, bf16[2,4,32,2048]{3,2,1,0:T(8,128)(2,1)}, u32[]{:S(2)}, u32[]{:S(2)}) collective-permute-start(bf16[2,4,32,2048]{3,2,1,0:T(8,128)(2,1)} %bitcast_dynamic-update-slice_fusion.24), channel_id=1, source_target_pairs={{0,8},{4,12},{8,0},{12,4},{16,24},{20,28},{24,16},{28,20},{1,9},{5... | collective-permute-start | bytes 3145736 | tf_op jit(solution)/shard_map/ppermute | solution.py:56
  191.3 44.7 %collective-permute-start.23 = (bf16[2,4,32,2048]{3,2,1,0:T(8,128)(2,1)}, bf16[2,4,32,2048]{3,2,1,0:T(8,128)(2,1)}, u32[]{:S(2)}, u32[]{:S(2)}) collective-permute-start(bf16[2,4,32,2048]{3,2,1,0:T(8,128)(2,1)} %bitcast_dynamic-update-slice_fusion.26), channel_id=1, source_target_pairs={{0,16},{4,20},{8,24},{12,28},{16,0},{20,4},{24,8},{28,12},{1,17},{... | collective-permute-start | bytes 3145736 | tf_op jit(solution)/shard_map/ppermute | solution.py:56
  195.1 55.3 %collective-permute-start.18 = (bf16[2,2,4,32,3072]{4,3,2,1,0:T(8,128)(2,1)}, bf16[2,2,4,32,3072]{4,3,2,1,0:T(8,128)(2,1)}, u32[]{:S(2)}, u32[]{:S(2)}) collective-permute-start(bf16[2,2,4,32,3072]{4,3,2,1,0:T(8,128)(2,1)} %pad_maximum_fusion.2), channel_id=1, source_target_pairs={{0,4},{4,0},{8,12},{12,8},{16,20},{20,16},{24,28},{28,24},{1,5},{5... | collective-permute-start | bytes 9437192 | tf_op jit(solution)/shard_map/ppermute | solution.py:56
  219.1 105.6 %collective-permute-start.34 = (bf16[2,2,4,128,1024]{4,3,2,1,0:T(8,128)(2,1)}, bf16[2,2,4,128,1024]{4,3,2,1,0:T(8,128)(2,1)}, u32[]{:S(2)}, u32[]{:S(2)}) collective-permute-start(bf16[2,2,4,128,1024]{4,3,2,1,0:T(8,128)(2,1)} %pad_maximum_fusion.1), channel_id=1, source_target_pairs={{0,4},{4,0},{8,12},{12,8},{16,20},{20,16},{24,28},{28,24},{1,5},{5... | collective-permute-start | bytes 12582920 | tf_op jit(solution)/shard_map/ppermute | solution.py:56
  239.6 70.1 %collective-permute-start.26 = (bf16[2,2,4,32,4096]{4,3,2,1,0:T(8,128)(2,1)}, bf16[2,2,4,32,4096]{4,3,2,1,0:T(8,128)(2,1)}, u32[]{:S(2)}, u32[]{:S(2)}) collective-permute-start(bf16[2,2,4,32,4096]{4,3,2,1,0:T(8,128)(2,1)} %pad_maximum_fusion), channel_id=1, source_target_pairs={{0,4},{4,0},{8,12},{12,8},{16,20},{20,16},{24,28},{28,24},{1,5},{5... | collective-permute-start | bytes 12582920 | tf_op jit(solution)/shard_map/ppermute | solution.py:56
  430.0 185.9 %collective-permute-start.68 = (bf16[2048,1024]{1,0:T(8,128)(2,1)}, bf16[2048,1024]{1,0:T(8,128)(2,1)}, u32[]{:S(2)}, u32[]{:S(2)}) collective-permute-start(bf16[2048,1024]{1,0:T(8,128)(2,1)} %convolution_convert_fusion.2), channel_id=1, source_target_pairs={{0,4},{4,0},{8,12},{12,8},{16,20},{20,16},{24,28},{28,24},{1,5},{5... | collective-permute-start | bytes 12582920 | tf_op jit(solution)/shard_map/ppermute | solution.py:56
  449.6 92.8 %collective-permute-start.52 = (bf16[512,1024]{1,0:T(8,128)(2,1)}, bf16[512,1024]{1,0:T(8,128)(2,1)}, u32[]{:S(2)}, u32[]{:S(2)}) collective-permute-start(bf16[512,1024]{1,0:T(8,128)(2,1)} %convolution_convert_fusion.3), channel_id=1, source_target_pairs={{0,4},{4,0},{8,12},{12,8},{16,20},{20,16},{24,28},{28,24},{1,5},{5... | collective-permute-start | bytes 3145736 | tf_op jit(solution)/shard_map/ppermute | solution.py:56
  454.2 77.8 %collective-permute-start.41 = (bf16[128,1024]{1,0:T(8,128)(2,1)}, bf16[128,1024]{1,0:T(8,128)(2,1)S(1)}, u32[]{:S(2)}, u32[]{:S(2)}) collective-permute-start(bf16[128,1024]{1,0:T(8,128)(2,1)} %get-tuple-element.92), channel_id=1, source_target_pairs={{0,1},{1,2},{2,3},{3,0},{4,5},{5,6},{6,7},{7,4},{8,9},{9,10},{10,1... | collective-permute-start | bytes 786440 | tf_op jit(solution)/shard_map/ppermute | solution.py:61
  469.4 112.3 %collective-permute-start.44 = (bf16[512,3072]{1,0:T(8,128)(2,1)}, bf16[512,3072]{1,0:T(8,128)(2,1)}, u32[]{:S(2)}, u32[]{:S(2)}) collective-permute-start(bf16[512,3072]{1,0:T(8,128)(2,1)} %convolution_convert_fusion.1), channel_id=1, source_target_pairs={{0,4},{4,0},{8,12},{12,8},{16,20},{20,16},{24,28},{28,24},{1,5},{5... | collective-permute-start | bytes 9437192 | tf_op jit(solution)/shard_map/ppermute | solution.py:56
  469.4 62.6 %collective-permute-start.42 = (bf16[128,1024]{1,0:T(8,128)(2,1)}, bf16[128,1024]{1,0:T(8,128)(2,1)}, u32[]{:S(2)}, u32[]{:S(2)}) collective-permute-start(bf16[128,1024]{1,0:T(8,128)(2,1)} %get-tuple-element.91), channel_id=1, source_target_pairs={{0,2},{1,3},{2,0},{3,1},{4,6},{5,7},{6,4},{7,5},{8,10},{9,11},{10,... | collective-permute-start | bytes 786440 | tf_op jit(solution)/shard_map/ppermute | solution.py:61
  541.4 82.2 %collective-permute-start.60 = (bf16[512,4096]{1,0:T(8,128)(2,1)}, bf16[512,4096]{1,0:T(8,128)(2,1)S(1)}, u32[]{:S(2)}, u32[]{:S(2)}) collective-permute-start(bf16[512,4096]{1,0:T(8,128)(2,1)} %convolution_convert_fusion), channel_id=1, source_target_pairs={{0,4},{4,0},{8,12},{12,8},{16,20},{20,16},{24,28},{28,24},{1,5},{5... | collective-permute-start | bytes 12582920 | tf_op jit(solution)/shard_map/ppermute | solution.py:56
  542.4 45.7 %collective-permute-start.37 = (bf16[128,1024]{1,0:T(8,128)(2,1)S(1)}, bf16[128,1024]{1,0:T(8,128)(2,1)S(1)}, u32[]{:S(2)}, u32[]{:S(2)}) collective-permute-start(bf16[128,1024]{1,0:T(8,128)(2,1)S(1)} %copy-done.64), channel_id=1, source_target_pairs={{0,3},{1,0},{2,1},{3,2},{4,7},{5,4},{6,5},{7,6},{8,11},{9,8},{10,9... | collective-permute-start | bytes 786440 | tf_op jit(solution)/shard_map/ppermute | solution.py:61
  621.2 28.2 %collective-permute-start.71 = (bf16[2,4,128,512]{3,2,1,0:T(8,128)(2,1)S(1)}, bf16[2,4,128,512]{3,2,1,0:T(8,128)(2,1)S(1)}, u32[]{:S(2)}, u32[]{:S(2)}) collective-permute-start(bf16[2,4,128,512]{3,2,1,0:T(8,128)(2,1)S(1)} %dynamic-slice_bitcast_fusion), channel_id=1, source_target_pairs={{0,16},{4,20},{8,24},{12,28},{16,0},{20,4},{24,8},{28,12},{1,17},{... | collective-permute-start | bytes 3145736 | tf_op jit(solution)/shard_map/ppermute | solution.py:56
  622.4 28.7 %collective-permute-start.69 = (bf16[2,4,128,512]{3,2,1,0:T(8,128)(2,1)S(1)}, bf16[2,4,128,512]{3,2,1,0:T(8,128)(2,1)S(1)}, u32[]{:S(2)}, u32[]{:S(2)}) collective-permute-start(bf16[2,4,128,512]{3,2,1,0:T(8,128)(2,1)S(1)} %dynamic-slice_bitcast_fusion.1), channel_id=1, source_target_pairs={{0,8},{4,12},{8,0},{12,4},{16,24},{20,28},{24,16},{28,20},{1,9},{5... | collective-permute-start | bytes 3145736 | tf_op jit(solution)/shard_map/ppermute | solution.py:56
  634.8 37.0 %collective-permute-start.63 = (bf16[2,4,32,2048]{3,2,1,0:T(8,128)(2,1)S(1)}, bf16[2,4,32,2048]{3,2,1,0:T(8,128)(2,1)S(1)}, u32[]{:S(2)}, u32[]{:S(2)}) collective-permute-start(bf16[2,4,32,2048]{3,2,1,0:T(8,128)(2,1)S(1)} %dynamic-slice_bitcast_fusion.2), channel_id=1, source_target_pairs={{0,16},{4,20},{8,24},{12,28},{16,0},{20,4},{24,8},{28,12},{1,17},{... | collective-permute-start | bytes 3145736 | tf_op jit(solution)/shard_map/ppermute | solution.py:56
  638.0 35.6 %collective-permute-start.61 = (bf16[2,4,32,2048]{3,2,1,0:T(8,128)(2,1)S(1)}, bf16[2,4,32,2048]{3,2,1,0:T(8,128)(2,1)S(1)}, u32[]{:S(2)}, u32[]{:S(2)}) collective-permute-start(bf16[2,4,32,2048]{3,2,1,0:T(8,128)(2,1)S(1)} %dynamic-slice_bitcast_fusion.3), channel_id=1, source_target_pairs={{0,8},{4,12},{8,0},{12,4},{16,24},{20,28},{24,16},{28,20},{1,9},{5... | collective-permute-start | bytes 3145736 | tf_op jit(solution)/shard_map/ppermute | solution.py:56
  649.8 29.6 %collective-permute-start.72 = (bf16[4,128,512]{2,1,0:T(8,128)(2,1)S(1)}, bf16[4,128,512]{2,1,0:T(8,128)(2,1)S(1)}, u32[]{:S(2)}, u32[]{:S(2)}) collective-permute-start(bf16[4,128,512]{2,1,0:T(8,128)(2,1)S(1)} %dynamic-slice_bitcast_fusion.6), channel_id=1, source_target_pairs={{0,8},{4,12},{8,0},{12,4},{16,24},{20,28},{24,16},{28,20},{1,9},{5... | collective-permute-start | bytes 1572872 | tf_op jit(solution)/shard_map/ppermute | solution.py:56
  651.4 28.2 %collective-permute-start.70 = (bf16[4,128,512]{2,1,0:T(8,128)(2,1)S(1)}, bf16[4,128,512]{2,1,0:T(8,128)(2,1)S(1)}, u32[]{:S(2)}, u32[]{:S(2)}) collective-permute-start(bf16[4,128,512]{2,1,0:T(8,128)(2,1)S(1)} %dynamic-slice_bitcast_fusion.7), channel_id=1, source_target_pairs={{0,16},{4,20},{8,24},{12,28},{16,0},{20,4},{24,8},{28,12},{1,17},{... | collective-permute-start | bytes 1572872 | tf_op jit(solution)/shard_map/ppermute | solution.py:56
  686.0 27.1 %collective-permute-start.66 = (bf16[32,4096]{1,0:T(8,128)(2,1)S(1)}, bf16[32,4096]{1,0:T(8,128)(2,1)S(1)}, u32[]{:S(2)}, u32[]{:S(2)}) collective-permute-start(bf16[32,4096]{1,0:T(8,128)(2,1)S(1)} %get-tuple-element.80), channel_id=1, source_target_pairs={{0,2},{1,3},{2,0},{3,1},{4,6},{5,7},{6,4},{7,5},{8,10},{9,11},{10,... | collective-permute-start | bytes 786440 | tf_op jit(solution)/shard_map/ppermute | solution.py:61
  (129 other events, 1825.5 us)
Sparse Core Ops, SparseCore 0:
  394.1 136.3 reduce-scatter.3

commit v2 on v1

--- a/solution.py
+++ b/solution.py
@@ -119,39 +119,46 @@
     return full.reshape(-1, columns)
 
 
-def scatter_product(left, right):
-    count, rows = left.shape
-    columns = right.shape[1]
-    n = lax.axis_size("ctx")
-    me = lax.axis_index("ctx")
+def scatter_cores(whole):
+    n = lax.axis_size("ctx")
     k = levels()
-    groups = 2 ** (k - 1)
-    each = rows // (2 * groups)
-    split = left.reshape(count, groups, 2, each)
-
-    def half(index):
-        part = pick(split, index, 2).reshape(count, groups * each)
-        return jnp.einsum("rd,re->de", part, right, preferred_element_type=jnp.float32)
-
-    got = swap(half(1 - own_bit(0)).astype(jnp.bfloat16), 0)
-    total = (half(own_bit(0)) + got.astype(jnp.float32)).astype(jnp.bfloat16)
-    total = total.reshape((2,) * (k - 1) + (n, each // n, columns))
-    bits = list(range(1, k))
-    cut = columns // 256 * 128
+    rows, columns = whole.shape
+    split = whole.reshape((2,) * k + (n, rows // (n * 2**k), columns))
+    got = swap(pick(split, 1 - own_bit(0), k - 1), 0)
+    mine = pick(split, own_bit(0), k - 1)
+    return (mine.astype(jnp.float32) + got.astype(jnp.float32)).astype(jnp.bfloat16)
+
+
+def scatter_planes(total):
+    bits = list(range(1, levels()))
+    cut = max(total.shape[-1] // 256 * 128, 128)
+    ways = [(bits, total[..., :cut])]
+    if total.shape[-1] > cut:
+        ways.append((bits[::-1], total[..., cut:]))
     halves = []
-    for order, part in ((bits, total[..., :cut]), (bits[::-1], total[..., cut:])):
+    for order, part in ways:
         left_bits = sorted(bits, reverse=True)
         for bit in order:
             axis = left_bits.index(bit)
             got = swap(pick(part, 1 - own_bit(bit), axis), bit)
-            part = (pick(part, own_bit(bit), axis).astype(jnp.float32) + got.astype(jnp.float32)).astype(jnp.bfloat16)
+            mine = pick(part, own_bit(bit), axis)
+            part = (mine.astype(jnp.float32) + got.astype(jnp.float32)).astype(jnp.bfloat16)
             left_bits.remove(bit)
         halves.append(part)
-    part = jnp.concatenate(halves, -1)
+    return jnp.concatenate(halves, -1) if len(halves) > 1 else halves[0]
+
+
+def scatter_last(part):
+    n = lax.axis_size("ctx")
+    me = lax.axis_index("ctx")
     out = pick(part, me).astype(jnp.float32)
     for by in range(1, n):
         out = out + shift(pick(part, (me + by) % n), by).astype(jnp.float32)
     return out
+
+
+def product(left, right):
+    return jnp.einsum("rd,re->de", left, right, preferred_element_type=jnp.float32).astype(jnp.bfloat16)
 
 
 def probabilities(queries, keys, first):
@@ -182,7 +189,7 @@
     o_ref[...] = jnp.concatenate(outs, 1).astype(o_ref.dtype)
 
 
-def attend_back_kernel(q_ref, k_ref, v_ref, g_ref, dq_ref, dk_ref, dv_ref):
+def attend_back_kernel(q_ref, k_ref, v_ref, g_ref, down_ref, up_ref, dq_ref, dk_ref, dv_ref):
     length = q_ref.shape[0]
     step = length // 2
     scale = HEAD_DIM ** (-0.5)
@@ -234,7 +241,7 @@
     )(mixed, mixed, mixed)
 
 
-def attend_back(mixed, grad):
+def attend_back(mixed, grad, down_part, up_part):
     length, columns = mixed.shape
     width = columns // 3
     pairs = width // 128
@@ -245,14 +252,14 @@
     return pl.pallas_call(
         attend_back_kernel,
         grid=(pairs,),
-        in_specs=[block(0), block(1), block(2), block(0)],
+        in_specs=[block(0), block(1), block(2), block(0)] + [pl.BlockSpec(memory_space=pl.ANY)] * 2,
         out_specs=[block(0)] * 3,
         out_shape=[jax.ShapeDtypeStruct((length, width), jnp.bfloat16)] * 3,
         compiler_params=pltpu.CompilerParams(vmem_limit_bytes=48 * 2**20),
         cost_estimate=pl.CostEstimate(
             flops=10 * length * length * width, bytes_accessed=14 * length * width, transcendentals=0
         ),
-    )(mixed, mixed, mixed, grad)
+    )(mixed, mixed, mixed, grad, down_part, up_part)
 
 
 def shards(
@@ -310,25 +317,29 @@
     result = middle + jnp.dot(active, full_down, preferred_element_type=jnp.float32) + table[7]
     layer_out = from_sequence((result * live).astype(jnp.bfloat16), sequence_order, slots)
     down_bias_grad = jnp.sum(grad_out.astype(jnp.float32), 0)
-    down_sum = scatter_product(active, grad_out)
+    down_part = scatter_planes(scatter_cores(product(active, grad_out)))
     grad_active = jnp.einsum("rd,fd->rf", grad_out, full_down, preferred_element_type=jnp.float32)
     grad_hidden = gelu_pull(grad_active)[0].astype(jnp.bfloat16)
     up_bias_grad = jnp.sum(grad_hidden.astype(jnp.float32), 0)
-    up_sum = scatter_product(normed2, grad_hidden)
+    up_part = scatter_cores(product(normed2, grad_hidden))
     grad_normed2 = jnp.einsum("rf,df->rd", grad_hidden, full_up, preferred_element_type=jnp.float32)
     back_middle, gain2_grad, shift2_grad = norm2_pull(grad_normed2)
     grad_middle = grad_out.astype(jnp.float32) + back_middle
     grad_branch = grad_middle.astype(jnp.bfloat16)
     proj_bias_grad = jnp.sum(grad_branch.astype(jnp.float32), 0)
-    proj_sum = scatter_product(attended, grad_branch)
+    proj_sum = scatter_last(scatter_planes(scatter_cores(product(attended, grad_branch))))
     grad_attended = jnp.einsum(
         "re,de->rd", grad_branch, full_proj, preferred_element_type=jnp.float32
     ).astype(jnp.bfloat16)
-    grad_queries, grad_keys, grad_values = attend_back(mixed, grad_attended)
+    grad_queries, grad_keys, grad_values = attend_back(
+        mixed, grad_attended, down_part, up_part
+    )
+    down_sum = scatter_last(down_part)
+    up_sum = scatter_last(scatter_planes(up_part))
     query_bias_grad = jnp.sum(grad_queries.astype(jnp.float32), 0)
     value_bias_grad = jnp.sum(grad_values.astype(jnp.float32), 0)
     grad_mixed = jnp.concatenate((grad_queries, grad_keys, grad_values), -1)
-    qkv_sum = scatter_product(normed, grad_mixed)
+    qkv_sum = scatter_last(scatter_planes(scatter_cores(product(normed, grad_mixed))))
     grad_normed = jnp.einsum("re,de->rd", grad_mixed, full_qkv, preferred_element_type=jnp.float32)
     back_tokens, gain1_grad, shift1_grad = norm_pull(grad_normed)
     token_grad = from_sequence(
@@ -347,7 +358,8 @@
         )
     )
     table_grad = jnp.concatenate((small_grads, up_bias_grad.reshape(-1, width)), 0)
-    table_sum = lax.psum_scatter(table_grad, ("dp", "ctx"), scatter_dimension=1, tiled=True)
+    table_rows = jnp.pad(table_grad.T.astype(jnp.bfloat16), ((0, 0), (0, pad - entries)))
+    table_sum = scatter_last(scatter_planes(scatter_cores(table_rows)))[:, :entries].T
     qkv_new, qkv_mean, qkv_square = adam_update(
         qkv_weight, qkv_first, qkv_second, qkv_sum, rate_matrix, weight_decay
     )

time: 730 us -> 655 us (0.90)
  local copies, waits for them, and re-layouts: 169 us -> 91.8 us
  starting transfers between devices: 95.3 us -> 149 us
  waiting for transfers between devices: 259 us -> 206 us
  other arithmetic: 39.2 us -> 61.2 us
  between operations: 30.7 us -> 17.3 us
    unnamed x2 -> x0, waiting for transfers between devices: 61.1 us -> none
    ppermute x36 -> x39, starting transfers between devices: 62.4 us -> 104 us  [shift(): return lax.ppermute(array, 'ctx', [(c, (c + by) % n) for c in range(n)])]
    unnamed x180 -> x170, local copies, waits for them, and re-layouts: 47.5 us -> 9.19 us
    ppermute x40 -> x43, waiting for transfers between devices: 116 us -> 139 us  [swap(): lax.ppermute(array, 'dp', [(d, d ^ 1 << bit) for d in range(lax.axis_size...]
    convert_element_type x17 -> x23, other arithmetic: 4.23 us -> 23.9 us  [the longest x5 16 us: scatter_cores(): (mine.astype(jnp.float32) + got.astype(jnp.float32)).astype(jnp.bfloat16)]
    dynamic_slice x3 -> x2, local copies, waits for them, and re-layouts: 19.3 us -> 1.04 us  [pick(): return lax.dynamic_index_in_dim(array, index, axis, keepdims=False)]
    ppermute x36 -> x39, waiting for transfers between devices: 82.6 us -> 67.3 us  [shift(): return lax.ppermute(array, 'ctx', [(c, (c + by) % n) for c in range(n)])]
    reshape x3 -> x4, local copies, waits for them, and re-layouts: 13 us -> 0.02 us  [layer_norm(): return center * lax.rsqrt(variance + norm_eps) * gain + shift]
  transfers between devices with their start and end apart: 77 -> 82, of which waited for: 35 -> 31; matrix products, arithmetic and copies ran while one was open for 33% -> 27% of each run, Pallas kernels for 2% -> 6%
where the time goes in v2:
time: 655 us; the launch traced here: 650 us
  waiting for transfers between devices  206 us (31%)
  starting transfers between devices  149 us (23%)
  local copies, waits for them, and re-layouts  91.8 us (14%)
  matrix products  83.2 us (13%)
  other arithmetic  61.2 us (9%)
  Pallas kernels  41.1 us (6%)
  between operations  17.3 us (3%)
    ppermute x43, waiting for transfers between devices, swap(): lax.ppermute(array, 'dp', [(d, d ^ 1 << bit) for d in range(lax.axis_size...  139 us
    ppermute x39, starting transfers between devices, shift(): return lax.ppermute(array, 'ctx', [(c, (c + by) % n) for c in range(n)])  104 us
    ppermute x39, waiting for transfers between devices, shift(): return lax.ppermute(array, 'ctx', [(c, (c + by) % n) for c in range(n)])  67.3 us
    ppermute x43, starting transfers between devices, swap(): lax.ppermute(array, 'dp', [(d, d ^ 1 << bit) for d in range(lax.axis_size...  45 us
    dynamic_update_slice x60, local copies, waits for them, and re-layouts, put(): return lax.dynamic_update_index_in_dim(array, piece, index, axis)  42.4 us
    pallas_call x1, Pallas kernels, attend_back(): pl.pallas_call(attend_back_kernel, grid=(pairs,), in_specs=[block(0), blo...  25 us
    dot_general x4, matrix products, product(): jnp.einsum('rd,re->de', left, right, preferred_element_type=jnp.float32)  23.6 us
    squeeze x26, local copies, waits for them, and re-layouts, pick(): return lax.dynamic_index_in_dim(array, index, axis, keepdims=False)  17.3 us
  transfers between devices with their start and end apart: 82, of which 31 were waited for; matrix products, arithmetic and copies ran while one was open for 27% of the time, Pallas kernels for 6%

profile of v2, /device:TPU:0, one launch (start us, length us, event | category | flops | bytes accessed | tf_op | source)
XLA Modules:
  0.0 649.6 jit_solution(17134713292411606505)
XLA Ops:
  59.8 7.4 %collective-permute-start.20 = (bf16[32,4096]{1,0:T(8,128)(2,1)S(1)}, bf16[32,4096]{1,0:T(8,128)(2,1)S(1)}, u32[]{:S(2)}, u32[]{:S(2)}) collective-permute-start(bf16[32,4096]{1,0:T(8,128)(2,1)S(1)} %copy-done.52), channel_id=1, source_target_pairs={{0,2},{1,3},{2,0},{3,1},{4,6},{5,7},{6,4},{7,5},{8,10},{9,11},{10,... | collective-permute-start | bytes 786440 | tf_op jit(solution)/shard_map/ppermute | solution.py:61
  70.7 12.1 %collective-permute-done.20 = bf16[32,4096]{1,0:T(8,128)(2,1)S(1)} collective-permute-done((bf16[32,4096]{1,0:T(8,128)(2,1)S(1)}, bf16[32,4096]{1,0:T(8,128)(2,1)S(1)}, u32[]{:S(2)}, u32[]{:S(2)}) %collective-permute-start.20) | collective-permute-done | bytes 262176 | tf_op jit(solution)/shard_map/ppermute | solution.py:61
  82.8 5.0 collective-permute-start
  98.2 9.3 %collective-permute-done.1 = bf16[128,1024]{1,0:T(8,128)(2,1)S(1)} collective-permute-done((bf16[128,1024]{1,0:T(8,128)(2,1)S(1)}, bf16[128,1024]{1,0:T(8,128)(2,1)S(1)}, u32[]{:S(2)}, u32[]{:S(2)}) %collective-permute-start.1) | collective-permute-done | bytes 262176 | tf_op jit(solution)/shard_map/ppermute | solution.py:61
  110.9 5.1 collective-permute-start.39
  124.8 5.6 collective-permute-done.39
  148.3 7.1 %collective-permute-done.24 = bf16[4,32,2048]{2,1,0:T(8,128)(2,1)S(1)} collective-permute-done((bf16[4,32,2048]{2,1,0:T(8,128)(2,1)S(1)}, bf16[4,32,2048]{2,1,0:T(8,128)(2,1)S(1)}, u32[]{:S(2)}, u32[]{:S(2)}) %collective-permute-start.24) | collective-permute-done | bytes 524320 | tf_op jit(solution)/shard_map/ppermute | solution.py:56
  170.7 9.7 %collective-permute-done.17 = bf16[2,4,32,1536]{3,2,1,0:T(8,128)(2,1)S(1)} collective-permute-done((bf16[2,4,32,1536]{3,2,1,0:T(8,128)(2,1)S(1)}, bf16[2,4,32,1536]{3,2,1,0:T(8,128)(2,1)S(1)}, u32[]{:S(2)}, u32[]{:S(2)}) %collective-permute-start.17) | collective-permute-done | bytes 786464 | tf_op jit(solution)/shard_map/ppermute | solution.py:56
  190.7 31.7 %collective-permute-done.25 = bf16[2,4,32,2048]{3,2,1,0:T(8,128)(2,1)} collective-permute-done((bf16[2,4,32,2048]{3,2,1,0:T(8,128)(2,1)}, bf16[2,4,32,2048]{3,2,1,0:T(8,128)(2,1)}, u32[]{:S(2)}, u32[]{:S(2)}) %collective-permute-start.25) | collective-permute-done | bytes 1048608 | tf_op jit(solution)/shard_map/ppermute | solution.py:56
  254.6 16.2 %shard_map.314 = bf16[512,1024]{1,0:T(8,128)(2,1)S(1)} custom-call(bf16[512,3072]{1,0:T(8,128)(2,1)S(1)} %add_convert_fusion.q_ref.k_ref.v_ref, bf16[512,3072]{1,0:T(8,128)(2,1)S(1)} %add_convert_fusion.q_ref.k_ref.v_ref, bf16[512,3072]{1,0:T(8,128)(2,1)S(1)} %add_convert_fusion.q_ref.k_ref.v_ref), custom_call_target="tpu_custom_call" | custom-call | flops 1073741824 | bytes 4194304 | tf_op jit(solution)/shard_map/pallas_call | solution.py:231
  277.2 10.9 %fusion.113 = f32[512,4096]{1,0:T(8,128)} fusion(bf16[1024,4096]{1,0:T(8,128)(2,1)} %bitcast.489, f32[512,1024]{1,0:T(8,128)S(1)} %get-tuple-element.166, f32[1024]{0:T(1024)S(1)} %get-tuple-element.66, f32[1024]{0:T(1024)S(1)} %get-tuple-element.64, f32[512]{0:T(512)S(1)} %fusion.109, f32[512]{0:T(512)S(1)} %broadcast_multiply_fusion), kind=kOutput, calls=%fused_computation.351 | convolution fusion | flops 4297588736 | bytes 18886656 | tf_op jit(solution)/shard_map/dot_general | solution.py:314
  288.1 13.4 %convolution_convert_fusion.1 = bf16[4096,1024]{1,0:T(8,128)(2,1)} fusion(bf16[512,1024]{1,0:T(8,128)(2,1)S(1)} %bitcast.477, f32[512,4096]{1,0:T(8,128)} %fusion.113, f32[4096]{0:T(1024)S(1)} %bitcast.513), kind=kOutput, calls=%fused_computation.16 | convolution fusion | flops 4320133120 | bytes 17842176 | tf_op jit(solution)/shard_map/rd,re->de/dot_general | solution.py:161
  304.4 15.0 %fusion.116 = (bf16[4096]{0:T(1024)(128)(2,1)S(1)}, bf16[512,4096]{1,0:T(8,128)(2,1)S(1)}) fusion(f32[512,4096]{1,0:T(8,128)} %fusion.113, f32[4096]{0:T(1024)S(1)} %bitcast.514, bf16[512,1024]{1,0:T(8,128)(2,1)S(1)} %bitcast.478, bf16[4096,1024]{1,0:T(8,128)(2,1)S(1)} %bitcast.487), kind=kOutput, calls=%fused_computation.353 | convolution fusion | flops 4349489152 | bytes 22044672 | tf_op jit(solution)/shard_map/rd,fd->rf/dot_general | solution.py:321
  319.3 9.5 %multiply_reduce_fusion = (bf16[1024]{0:T(1024)(128)(2,1)S(1)}, f32[512]{0:T(512)S(1)}, bf16[1024]{0:T(1024)(128)(2,1)S(1)}, f32[512,1024]{1,0:T(8,128)}) fusion(f32[512,1024]{1,0:T(8,128)S(1)} %get-tuple-element.166, f32[512]{0:T(512)S(1)} %fusion.109, f32[512]{0:T(512)S(1)} %broadcast_multiply_fusion, f32[1024]{0:T(1024)S(1)} %get-tuple-element.64, ...), kind=kOutput, calls=%fused_computation.65 | convolution fusion | flops 4299159040 | bytes 16791552 | tf_op jit(solution)/shard_map/rf,df->rd/dot_general | solution.py:325
  328.9 5.1 convolution_convert_fusion
  334.0 14.2 %multiply_convert_fusion.2 = bf16[512,1024]{1,0:T(8,128)(2,1)S(1)} fusion(f32[512,1024]{1,0:T(8,128)S(1)} %get-tuple-element.166, bf16[4096,1024]{1,0:T(8,128)(2,1)} %bitcast.488, f32[]{:T(128)S(6)} %select_n.693, f32[1024]{0:T(1024)S(1)} %get-tuple-element.65, f32[512,4096]{1,0:T(8,128)} %fusion.113, f32[4096]{0:T(1024)S(1)} %bitcast.515), kind=kOutput, calls=%fused_computation.70 | convolution fusion | flops 4318035968 | bytes 19943428 | tf_op jit(solution)/shard_map/dot_general | solution.py:317
  372.2 7.8 %collective-permute-done.36 = bf16[128,1024]{1,0:T(8,128)(2,1)} collective-permute-done((bf16[128,1024]{1,0:T(8,128)(2,1)}, bf16[128,1024]{1,0:T(8,128)(2,1)}, u32[]{:S(2)}, u32[]{:S(2)}) %collective-permute-start.36) | collective-permute-done | bytes 262176 | tf_op jit(solution)/shard_map/ppermute | solution.py:61
  384.0 7.0 %collective-permute-done.61 = bf16[2,4,32,512]{3,2,1,0:T(8,128)(2,1)S(1)} collective-permute-done((bf16[2,4,32,512]{3,2,1,0:T(8,128)(2,1)S(1)}, bf16[2,4,32,512]{3,2,1,0:T(8,128)(2,1)S(1)}, u32[]{:S(2)}, u32[]{:S(2)}) %collective-permute-start.61) | collective-permute-done | bytes 262176 | tf_op jit(solution)/shard_map/ppermute | solution.py:56
  396.2 5.9 collective-permute-start.65
  409.0 5.8 fusion.7
  427.8 15.1 %collective-permute-done.44 = bf16[2,4,128,512]{3,2,1,0:T(8,128)(2,1)} collective-permute-done((bf16[2,4,128,512]{3,2,1,0:T(8,128)(2,1)}, bf16[2,4,128,512]{3,2,1,0:T(8,128)(2,1)}, u32[]{:S(2)}, u32[]{:S(2)}) %collective-permute-start.44) | collective-permute-done | bytes 1048608 | tf_op jit(solution)/shard_map/ppermute | solution.py:56
  449.3 18.6 %collective-permute-done.66 = bf16[2,4,32,2048]{3,2,1,0:T(8,128)(2,1)S(1)} collective-permute-done((bf16[2,4,32,2048]{3,2,1,0:T(8,128)(2,1)S(1)}, bf16[2,4,32,2048]{3,2,1,0:T(8,128)(2,1)S(1)}, u32[]{:S(2)}, u32[]{:S(2)}) %collective-permute-start.66) | collective-permute-done | bytes 1048608 | tf_op jit(solution)/shard_map/ppermute | solution.py:56
  472.4 5.7 collective-permute-done.45
  478.7 25.0 %shard_map.315 = (bf16[512,1024]{1,0:T(8,128)(2,1)S(1)}, bf16[512,1024]{1,0:T(8,128)(2,1)S(1)}, bf16[512,1024]{1,0:T(8,128)(2,1)S(1)}) custom-call(bf16[512,3072]{1,0:T(8,128)(2,1)} %copy-done, bf16[512,3072]{1,0:T(8,128)(2,1)} %copy-done, bf16[512,3072]{1,0:T(8,128)(2,1)} %copy-done, bf16[512,1024]{1,0:T(8,128)(2,1)S(1)} %fusion.36.g_ref, ...), custom_call_target="tpu_custom_call" | custom-call | flops 2684354560 | bytes 7340032 | tf_op jit(solution)/shard_map/pallas_call | solution.py:252
  528.7 6.1 collective-permute-done.77
  546.5 6.9 %collective-permute-start.79 = (bf16[32,128]{0,1:T(8,128)(2,1)S(1)}, bf16[32,128]{0,1:T(8,128)(2,1)S(1)}, u32[]{:S(2)}, u32[]{:S(2)}) collective-permute-start(bf16[32,128]{0,1:T(8,128)(2,1)S(1)} %get-tuple-element.153), channel_id=1, source_target_pairs={{0,1},{1,2},{2,3},{3,0},{4,5},{5,6},{6,7},{7,4},{8,9},{9,10},{10,1... | collective-permute-start | bytes 24584 | tf_op jit(solution)/shard_map/ppermute | solution.py:61
  553.6 8.5 %collective-permute-done.79 = bf16[32,128]{0,1:T(8,128)(2,1)S(1)} collective-permute-done((bf16[32,128]{0,1:T(8,128)(2,1)S(1)}, bf16[32,128]{0,1:T(8,128)(2,1)S(1)}, u32[]{:S(2)}, u32[]{:S(2)}) %collective-permute-start.79) | collective-permute-done | bytes 8224 | tf_op jit(solution)/shard_map/ppermute | solution.py:61
  562.1 5.7 collective-permute-start.47
  570.3 10.0 %collective-permute-done.71 = bf16[32,4096]{1,0:T(8,128)(2,1)S(1)} collective-permute-done((bf16[32,4096]{1,0:T(8,128)(2,1)S(1)}, bf16[32,4096]{1,0:T(8,128)(2,1)S(1)}, u32[]{:S(2)}, u32[]{:S(2)}) %collective-permute-start.71) | collective-permute-done | bytes 262176 | tf_op jit(solution)/shard_map/ppermute | solution.py:61
  590.7 14.4 %collective-permute-start.73 = (bf16[128,1024]{1,0:T(8,128)(2,1)S(1)}, bf16[128,1024]{1,0:T(8,128)(2,1)S(1)}, u32[]{:S(2)}, u32[]{:S(2)}) collective-permute-start(bf16[128,1024]{1,0:T(8,128)(2,1)S(1)} %get-tuple-element.112), channel_id=1, source_target_pairs={{0,1},{1,2},{2,3},{3,0},{4,5},{5,6},{6,7},{7,4},{8,9},{9,10},{10,1... | collective-permute-start | bytes 786440 | tf_op jit(solution)/shard_map/ppermute | solution.py:61
  609.2 16.5 %collective-permute-done.53 = bf16[2,4,32,1536]{3,2,1,0:T(8,128)(2,1)S(1)} collective-permute-done((bf16[2,4,32,1536]{3,2,1,0:T(8,128)(2,1)S(1)}, bf16[2,4,32,1536]{3,2,1,0:T(8,128)(2,1)S(1)}, u32[]{:S(2)}, u32[]{:S(2)}) %collective-permute-start.53) | collective-permute-done | bytes 786464 | tf_op jit(solution)/shard_map/ppermute | solution.py:56
  641.6 6.3 collective-permute-done.56
  (532 shorter events, 289.7 us)
Async XLA Ops:
  2.5 32.2 %collective-permute-start.3 = (bf16[32,1152]{1,0:T(8,128)(2,1)S(1)}, bf16[32,1152]{1,0:T(8,128)(2,1)}, u32[]{:S(2)}, u32[]{:S(2)}) collective-permute-start(bf16[32,1152]{1,0:T(8,128)(2,1)S(1)} %fusion.92), channel_id=1, source_target_pairs={{0,1},{1,2},{2,3},{3,0},{4,5},{5,6},{6,7},{7,4},{8,9},{9,10},{10,1... | collective-permute-start | bytes 221192 | tf_op jit(solution)/shard_map/ppermute | solution.py:61
  5.5 32.9 %collective-permute-start.4 = (bf16[32,1152]{1,0:T(8,128)(2,1)S(1)}, bf16[32,1152]{1,0:T(8,128)(2,1)}, u32[]{:S(2)}, u32[]{:S(2)}) collective-permute-start(bf16[32,1152]{1,0:T(8,128)(2,1)S(1)} %fusion.92), channel_id=1, source_target_pairs={{0,2},{1,3},{2,0},{3,1},{4,6},{5,7},{6,4},{7,5},{8,10},{9,11},{10,... | collective-permute-start | bytes 221192 | tf_op jit(solution)/shard_map/ppermute | solution.py:61
  8.1 31.8 %collective-permute-start.5 = (bf16[32,1152]{1,0:T(8,128)(2,1)S(1)}, bf16[32,1152]{1,0:T(8,128)(2,1)}, u32[]{:S(2)}, u32[]{:S(2)}) collective-permute-start(bf16[32,1152]{1,0:T(8,128)(2,1)S(1)} %fusion.92), channel_id=1, source_target_pairs={{0,3},{1,0},{2,1},{3,2},{4,7},{5,4},{6,5},{7,6},{8,11},{9,8},{10,9... | collective-permute-start | bytes 221192 | tf_op jit(solution)/shard_map/ppermute | solution.py:61
  12.3 30.3 %collective-permute-start.11 = (bf16[32,3072]{1,0:T(8,128)(2,1)}, bf16[32,3072]{1,0:T(8,128)(2,1)}, u32[]{:S(2)}, u32[]{:S(2)}) collective-permute-start(bf16[32,3072]{1,0:T(8,128)(2,1)} %get-tuple-element.100), channel_id=1, source_target_pairs={{0,1},{1,2},{2,3},{3,0},{4,5},{5,6},{6,7},{7,4},{8,9},{9,10},{10,1... | collective-permute-start | bytes 589832 | tf_op jit(solution)/shard_map/ppermute | solution.py:61
  12.9 34.2 %collective-permute-start.12 = (bf16[32,3072]{1,0:T(8,128)(2,1)}, bf16[32,3072]{1,0:T(8,128)(2,1)}, u32[]{:S(2)}, u32[]{:S(2)}) collective-permute-start(bf16[32,3072]{1,0:T(8,128)(2,1)} %get-tuple-element.100), channel_id=1, source_target_pairs={{0,2},{1,3},{2,0},{3,1},{4,6},{5,7},{6,4},{7,5},{8,10},{9,11},{10,... | collective-permute-start | bytes 589832 | tf_op jit(solution)/shard_map/ppermute | solution.py:61
  38.4 77.8 %collective-permute-start.27 = (bf16[128,1024]{1,0:T(8,128)(2,1)S(1)}, bf16[128,1024]{1,0:T(8,128)(2,1)S(1)}, u32[]{:S(2)}, u32[]{:S(2)}) collective-permute-start(bf16[128,1024]{1,0:T(8,128)(2,1)S(1)} %copy-done.51), channel_id=1, source_target_pairs={{0,1},{1,2},{2,3},{3,0},{4,5},{5,6},{6,7},{7,4},{8,9},{9,10},{10,1... | collective-permute-start | bytes 786440 | tf_op jit(solution)/shard_map/ppermute | solution.py:61
  39.9 78.1 %collective-permute-start.28 = (bf16[128,1024]{1,0:T(8,128)(2,1)S(1)}, bf16[128,1024]{1,0:T(8,128)(2,1)S(1)}, u32[]{:S(2)}, u32[]{:S(2)}) collective-permute-start(bf16[128,1024]{1,0:T(8,128)(2,1)S(1)} %copy-done.51), channel_id=1, source_target_pairs={{0,2},{1,3},{2,0},{3,1},{4,6},{5,7},{6,4},{7,5},{8,10},{9,11},{10,... | collective-permute-start | bytes 786440 | tf_op jit(solution)/shard_map/ppermute | solution.py:61
  42.5 78.1 %collective-permute-start.29 = (bf16[128,1024]{1,0:T(8,128)(2,1)S(1)}, bf16[128,1024]{1,0:T(8,128)(2,1)S(1)}, u32[]{:S(2)}, u32[]{:S(2)}) collective-permute-start(bf16[128,1024]{1,0:T(8,128)(2,1)S(1)} %copy-done.51), channel_id=1, source_target_pairs={{0,3},{1,0},{2,1},{3,2},{4,7},{5,4},{6,5},{7,6},{8,11},{9,8},{10,9... | collective-permute-start | bytes 786440 | tf_op jit(solution)/shard_map/ppermute | solution.py:61
  144.4 42.0 %collective-permute-start.10 = (bf16[2,2,4,32,1152]{4,3,2,1,0:T(8,128)(2,1)S(1)}, bf16[2,2,4,32,1152]{4,3,2,1,0:T(8,128)(2,1)S(1)}, u32[]{:S(2)}, u32[]{:S(2)}) collective-permute-start(bf16[2,2,4,32,1152]{4,3,2,1,0:T(8,128)(2,1)S(1)} %pad_maximum_fusion.4), channel_id=1, source_target_pairs={{0,4},{4,0},{8,12},{12,8},{16,20},{20,16},{24,28},{28,24},{1,5},{5... | collective-permute-start | bytes 3538952 | tf_op jit(solution)/shard_map/ppermute | solution.py:56
  147.0 33.4 %collective-permute-start.17 = (bf16[2,4,32,1536]{3,2,1,0:T(8,128)(2,1)S(1)}, bf16[2,4,32,1536]{3,2,1,0:T(8,128)(2,1)S(1)}, u32[]{:S(2)}, u32[]{:S(2)}) collective-permute-start(bf16[2,4,32,1536]{3,2,1,0:T(8,128)(2,1)S(1)} %bitcast_dynamic-update-slice_fusion.28), channel_id=1, source_target_pairs={{0,8},{4,12},{8,0},{12,4},{16,24},{20,28},{24,16},{28,20},{1,9},{5... | collective-permute-start | bytes 2359304 | tf_op jit(solution)/shard_map/ppermute | solution.py:56
  157.9 72.3 %collective-permute-start.33 = (bf16[2,4,128,512]{3,2,1,0:T(8,128)(2,1)}, bf16[2,4,128,512]{3,2,1,0:T(8,128)(2,1)}, u32[]{:S(2)}, u32[]{:S(2)}) collective-permute-start(bf16[2,4,128,512]{3,2,1,0:T(8,128)(2,1)} %bitcast_dynamic-update-slice_fusion.20), channel_id=1, source_target_pairs={{0,8},{4,12},{8,0},{12,4},{16,24},{20,28},{24,16},{28,20},{1,9},{5... | collective-permute-start | bytes 3145736 | tf_op jit(solution)/shard_map/ppermute | solution.py:56
  163.6 67.9 %collective-permute-start.31 = (bf16[2,4,128,512]{3,2,1,0:T(8,128)(2,1)}, bf16[2,4,128,512]{3,2,1,0:T(8,128)(2,1)}, u32[]{:S(2)}, u32[]{:S(2)}) collective-permute-start(bf16[2,4,128,512]{3,2,1,0:T(8,128)(2,1)} %bitcast_dynamic-update-slice_fusion.22), channel_id=1, source_target_pairs={{0,16},{4,20},{8,24},{12,28},{16,0},{20,4},{24,8},{28,12},{1,17},{... | collective-permute-start | bytes 3145736 | tf_op jit(solution)/shard_map/ppermute | solution.py:56
  180.4 42.0 %collective-permute-start.25 = (bf16[2,4,32,2048]{3,2,1,0:T(8,128)(2,1)}, bf16[2,4,32,2048]{3,2,1,0:T(8,128)(2,1)}, u32[]{:S(2)}, u32[]{:S(2)}) collective-permute-start(bf16[2,4,32,2048]{3,2,1,0:T(8,128)(2,1)} %bitcast_dynamic-update-slice_fusion.24), channel_id=1, source_target_pairs={{0,8},{4,12},{8,0},{12,4},{16,24},{20,28},{24,16},{28,20},{1,9},{5... | collective-permute-start | bytes 3145736 | tf_op jit(solution)/shard_map/ppermute | solution.py:56
  181.1 42.7 %collective-permute-start.23 = (bf16[2,4,32,2048]{3,2,1,0:T(8,128)(2,1)}, bf16[2,4,32,2048]{3,2,1,0:T(8,128)(2,1)}, u32[]{:S(2)}, u32[]{:S(2)}) collective-permute-start(bf16[2,4,32,2048]{3,2,1,0:T(8,128)(2,1)} %bitcast_dynamic-update-slice_fusion.26), channel_id=1, source_target_pairs={{0,16},{4,20},{8,24},{12,28},{16,0},{20,4},{24,8},{28,12},{1,17},{... | collective-permute-start | bytes 3145736 | tf_op jit(solution)/shard_map/ppermute | solution.py:56
  186.4 58.2 %collective-permute-start.18 = (bf16[2,2,4,32,3072]{4,3,2,1,0:T(8,128)(2,1)}, bf16[2,2,4,32,3072]{4,3,2,1,0:T(8,128)(2,1)}, u32[]{:S(2)}, u32[]{:S(2)}) collective-permute-start(bf16[2,2,4,32,3072]{4,3,2,1,0:T(8,128)(2,1)} %pad_maximum_fusion.2), channel_id=1, source_target_pairs={{0,4},{4,0},{8,12},{12,8},{16,20},{20,16},{24,28},{28,24},{1,5},{5... | collective-permute-start | bytes 9437192 | tf_op jit(solution)/shard_map/ppermute | solution.py:56
  230.1 42.4 %collective-permute-start.26 = (bf16[2,2,4,32,4096]{4,3,2,1,0:T(8,128)(2,1)}, bf16[2,2,4,32,4096]{4,3,2,1,0:T(8,128)(2,1)}, u32[]{:S(2)}, u32[]{:S(2)}) collective-permute-start(bf16[2,2,4,32,4096]{4,3,2,1,0:T(8,128)(2,1)} %pad_maximum_fusion), channel_id=1, source_target_pairs={{0,4},{4,0},{8,12},{12,8},{16,20},{20,16},{24,28},{28,24},{1,5},{5... | collective-permute-start | bytes 12582920 | tf_op jit(solution)/shard_map/ppermute | solution.py:56
  235.4 66.1 %collective-permute-start.34 = (bf16[2,2,4,128,1024]{4,3,2,1,0:T(8,128)(2,1)}, bf16[2,2,4,128,1024]{4,3,2,1,0:T(8,128)(2,1)}, u32[]{:S(2)}, u32[]{:S(2)}) collective-permute-start(bf16[2,2,4,128,1024]{4,3,2,1,0:T(8,128)(2,1)} %pad_maximum_fusion.1), channel_id=1, source_target_pairs={{0,4},{4,0},{8,12},{12,8},{16,20},{20,16},{24,28},{28,24},{1,5},{5... | collective-permute-start | bytes 12582920 | tf_op jit(solution)/shard_map/ppermute | solution.py:56
  357.2 51.9 %collective-permute-start.41 = (bf16[2,2,4,128,1024]{4,3,2,1,0:T(8,128)(2,1)}, bf16[2,2,4,128,1024]{4,3,2,1,0:T(8,128)(2,1)}, u32[]{:S(2)}, u32[]{:S(2)}) collective-permute-start(bf16[2,2,4,128,1024]{4,3,2,1,0:T(8,128)(2,1)} %dynamic-slice_bitcast_fusion.1), channel_id=1, source_target_pairs={{0,4},{4,0},{8,12},{12,8},{16,20},{20,16},{24,28},{28,24},{1,5},{5... | collective-permute-start | bytes 12582920 | tf_op jit(solution)/shard_map/ppermute | solution.py:56
  363.2 57.5 %collective-permute-start.46 = (bf16[2,2,4,32,4096]{4,3,2,1,0:T(8,128)(2,1)}, bf16[2,2,4,32,4096]{4,3,2,1,0:T(8,128)(2,1)}, u32[]{:S(2)}, u32[]{:S(2)}) collective-permute-start(bf16[2,2,4,32,4096]{4,3,2,1,0:T(8,128)(2,1)} %dynamic-slice_bitcast_fusion), channel_id=1, source_target_pairs={{0,4},{4,0},{8,12},{12,8},{16,20},{20,16},{24,28},{28,24},{1,5},{5... | collective-permute-start | bytes 12582920 | tf_op jit(solution)/shard_map/ppermute | solution.py:56
  365.6 36.4 %collective-permute-start.37 = (bf16[128,1024]{1,0:T(8,128)(2,1)}, bf16[128,1024]{1,0:T(8,128)(2,1)S(1)}, u32[]{:S(2)}, u32[]{:S(2)}) collective-permute-start(bf16[128,1024]{1,0:T(8,128)(2,1)} %get-tuple-element.128), channel_id=1, source_target_pairs={{0,3},{1,0},{2,1},{3,2},{4,7},{5,4},{6,5},{7,6},{8,11},{9,8},{10,9... | collective-permute-start | bytes 786440 | tf_op jit(solution)/shard_map/ppermute | solution.py:61
  426.6 41.4 %collective-permute-start.66 = (bf16[2,4,32,2048]{3,2,1,0:T(8,128)(2,1)S(1)}, bf16[2,4,32,2048]{3,2,1,0:T(8,128)(2,1)S(1)}, u32[]{:S(2)}, u32[]{:S(2)}) collective-permute-start(bf16[2,4,32,2048]{3,2,1,0:T(8,128)(2,1)S(1)} %dynamic-slice_bitcast_fusion.4), channel_id=1, source_target_pairs={{0,8},{4,12},{8,0},{12,4},{16,24},{20,28},{24,16},{28,20},{1,9},{5... | collective-permute-start | bytes 3145736 | tf_op jit(solution)/shard_map/ppermute | solution.py:56
  427.3 42.4 %collective-permute-start.68 = (bf16[2,4,32,2048]{3,2,1,0:T(8,128)(2,1)S(1)}, bf16[2,4,32,2048]{3,2,1,0:T(8,128)(2,1)S(1)}, u32[]{:S(2)}, u32[]{:S(2)}) collective-permute-start(bf16[2,4,32,2048]{3,2,1,0:T(8,128)(2,1)S(1)} %dynamic-slice_bitcast_fusion.3), channel_id=1, source_target_pairs={{0,16},{4,20},{8,24},{12,28},{16,0},{20,4},{24,8},{28,12},{1,17},{... | collective-permute-start | bytes 3145736 | tf_op jit(solution)/shard_map/ppermute | solution.py:56
  444.5 33.7 %collective-permute-start.45 = (bf16[4,128,512]{2,1,0:T(8,128)(2,1)S(1)}, bf16[4,128,512]{2,1,0:T(8,128)(2,1)S(1)}, u32[]{:S(2)}, u32[]{:S(2)}) collective-permute-start(bf16[4,128,512]{2,1,0:T(8,128)(2,1)S(1)} %dynamic-slice_bitcast_fusion.12), channel_id=1, source_target_pairs={{0,8},{4,12},{8,0},{12,4},{16,24},{20,28},{24,16},{28,20},{1,9},{5... | collective-permute-start | bytes 1572872 | tf_op jit(solution)/shard_map/ppermute | solution.py:56
  447.6 30.7 %collective-permute-start.43 = (bf16[4,128,512]{2,1,0:T(8,128)(2,1)S(1)}, bf16[4,128,512]{2,1,0:T(8,128)(2,1)S(1)}, u32[]{:S(2)}, u32[]{:S(2)}) collective-permute-start(bf16[4,128,512]{2,1,0:T(8,128)(2,1)S(1)} %dynamic-slice_bitcast_fusion.13), channel_id=1, source_target_pairs={{0,16},{4,20},{8,24},{12,28},{16,0},{20,4},{24,8},{28,12},{1,17},{... | collective-permute-start | bytes 1572872 | tf_op jit(solution)/shard_map/ppermute | solution.py:56
  469.2 50.8 %collective-permute-start.67 = (bf16[4,32,2048]{2,1,0:T(8,128)(2,1)}, bf16[4,32,2048]{2,1,0:T(8,128)(2,1)}, u32[]{:S(2)}, u32[]{:S(2)}) collective-permute-start(bf16[4,32,2048]{2,1,0:T(8,128)(2,1)} %dynamic-slice_bitcast_fusion.11), channel_id=1, source_target_pairs={{0,16},{4,20},{8,24},{12,28},{16,0},{20,4},{24,8},{28,12},{1,17},{... | collective-permute-start | bytes 1572872 | tf_op jit(solution)/shard_map/ppermute | solution.py:56
  470.9 50.4 %collective-permute-start.69 = (bf16[4,32,2048]{2,1,0:T(8,128)(2,1)}, bf16[4,32,2048]{2,1,0:T(8,128)(2,1)}, u32[]{:S(2)}, u32[]{:S(2)}) collective-permute-start(bf16[4,32,2048]{2,1,0:T(8,128)(2,1)} %dynamic-slice_bitcast_fusion.10), channel_id=1, source_target_pairs={{0,8},{4,12},{8,0},{12,4},{16,24},{20,28},{24,16},{28,20},{1,9},{5... | collective-permute-start | bytes 1572872 | tf_op jit(solution)/shard_map/ppermute | solution.py:56
  518.1 64.5 %collective-permute-start.50 = (bf16[2,2,4,32,3072]{4,3,2,1,0:T(8,128)(2,1)}, bf16[2,2,4,32,3072]{4,3,2,1,0:T(8,128)(2,1)}, u32[]{:S(2)}, u32[]{:S(2)}) collective-permute-start(bf16[2,2,4,32,3072]{4,3,2,1,0:T(8,128)(2,1)} %dynamic-slice_bitcast_fusion.2), channel_id=1, source_target_pairs={{0,4},{4,0},{8,12},{12,8},{16,20},{20,16},{24,28},{28,24},{1,5},{5... | collective-permute-start | bytes 9437192 | tf_op jit(solution)/shard_map/ppermute | solution.py:56
  545.0 35.4 %collective-permute-start.71 = (bf16[32,4096]{1,0:T(8,128)(2,1)S(1)}, bf16[32,4096]{1,0:T(8,128)(2,1)S(1)}, u32[]{:S(2)}, u32[]{:S(2)}) collective-permute-start(bf16[32,4096]{1,0:T(8,128)(2,1)S(1)} %copy-done.56), channel_id=1, source_target_pairs={{0,2},{1,3},{2,0},{3,1},{4,6},{5,7},{6,4},{7,5},{8,10},{9,11},{10,... | collective-permute-start | bytes 786440 | tf_op jit(solution)/shard_map/ppermute | solution.py:61
  545.0 35.4 %collective-permute-start.70 = (bf16[32,4096]{1,0:T(8,128)(2,1)S(1)}, bf16[32,4096]{1,0:T(8,128)(2,1)S(1)}, u32[]{:S(2)}, u32[]{:S(2)}) collective-permute-start(bf16[32,4096]{1,0:T(8,128)(2,1)S(1)} %get-tuple-element.115), channel_id=1, source_target_pairs={{0,1},{1,2},{2,3},{3,0},{4,5},{5,6},{6,7},{7,4},{8,9},{9,10},{10,1... | collective-permute-start | bytes 786440 | tf_op jit(solution)/shard_map/ppermute | solution.py:61
  580.4 57.2 %collective-permute-start.75 = (bf16[128,1024]{1,0:T(8,128)(2,1)S(1)}, bf16[128,1024]{1,0:T(8,128)(2,1)S(1)}, u32[]{:S(2)}, u32[]{:S(2)}) collective-permute-start(bf16[128,1024]{1,0:T(8,128)(2,1)S(1)} %get-tuple-element.114), channel_id=1, source_target_pairs={{0,3},{1,0},{2,1},{3,2},{4,7},{5,4},{6,5},{7,6},{8,11},{9,8},{10,9... | collective-permute-start | bytes 786440 | tf_op jit(solution)/shard_map/ppermute | solution.py:61
  582.6 57.0 %collective-permute-start.74 = (bf16[128,1024]{1,0:T(8,128)(2,1)S(1)}, bf16[128,1024]{1,0:T(8,128)(2,1)S(1)}, u32[]{:S(2)}, u32[]{:S(2)}) collective-permute-start(bf16[128,1024]{1,0:T(8,128)(2,1)S(1)} %get-tuple-element.113), channel_id=1, source_target_pairs={{0,2},{1,3},{2,0},{3,1},{4,6},{5,7},{6,4},{7,5},{8,10},{9,11},{10,... | collective-permute-start | bytes 786440 | tf_op jit(solution)/shard_map/ppermute | solution.py:61
  590.7 48.9 %collective-permute-start.73 = (bf16[128,1024]{1,0:T(8,128)(2,1)S(1)}, bf16[128,1024]{1,0:T(8,128)(2,1)S(1)}, u32[]{:S(2)}, u32[]{:S(2)}) collective-permute-start(bf16[128,1024]{1,0:T(8,128)(2,1)S(1)} %get-tuple-element.112), channel_id=1, source_target_pairs={{0,1},{1,2},{2,3},{3,0},{4,5},{5,6},{6,7},{7,4},{8,9},{9,10},{10,1... | collective-permute-start | bytes 786440 | tf_op jit(solution)/shard_map/ppermute | solution.py:61
  (132 other events, 1984.6 us)
